TPU v7x, 512 devices: a whole 4x8x8 slice. The times are simulated.
512 devices in a mesh: lat: 64 (over z, x, y_hi), lon: 8 (over y_lo, core).
Axes of the slice: x: 4, y: 8 (y_hi: 2, y_lo: 4; y = y_hi * 4 + y_lo), z: 8, core: 2. Of those that a mesh axis runs over, the one named last changes fastest.
Arguments:
- elevation: float32 [1, 3072, 8640], P(None, 'lat', 'lon'), may hold values from -30 to 30
- velocity: float32 [1, 2, 3072, 8640], P(None, None, 'lat', 'lon'), may hold values from -3 to 3
- wind_forcing: float32 [2, 3072, 8640], P(None, 'lat', 'lon'), may hold values from -0.6 to 0.6
- ocean_depth: float32 [3072, 8640], P('lat', 'lon'), may hold values from 0.2 to 1
- wet_mask: int32 [3072, 8640], P('lat', 'lon'), may hold values from 0 to 1, as said below
- love_factor: float32 [1081], replicated, may hold values from 0.3 to 3
- wavenumbers: int32 [64], replicated, may hold values from 0 to 127, as said below
Outputs:
- new_elevation: float32 [1, 3072, 8640], P(None, 'lat', 'lon')
- new_velocity: float32 [1, 2, 3072, 8640], P(None, None, 'lat', 'lon')
- self_loading: float32 [1, 3072, 8640], P(None, 'lat', 'lon')
Inputs may be any that keep to these rules, and one draw needn't show every extreme that they name: `wet_mask`: 0 in the 24 rows nearest each pole. `wavenumbers`: distinct.
All inputs are finite; a program needn't handle non-finite values.
Results may differ from a plain program's by a relative error of at most 0.0003.
Values sent between devices are 32-bit elements; how exact they have to be, the bound alone decides.
A program may use at most 64 MiB of HBM per device.

v0:
```python
import jax
import jax.numpy as jnp
from jax import lax
from jax.sharding import PartitionSpec as P

GRID_LAT = 3072
GRID_LON = 8640
DEGREES = 1081


friction_rate = 0.1
step_ratio = 0.05
highest = lax.Precision.HIGHEST


def with_halo(block, sides, width):
    for axis, dim in sides:
        count = lax.axis_size(axis)
        forward = [(i, i + 1) for i in range(count - 1)]
        forward.append((count - 1, 0))
        backward = [(target, source) for source, target in forward]
        low = lax.ppermute(
            lax.slice_in_dim(block, block.shape[dim] - width, None, axis=dim), axis, forward
        )
        high = lax.ppermute(lax.slice_in_dim(block, 0, width, axis=dim), axis, backward)
        block = jnp.concatenate([low, block, high], axis=dim)
    return block


def colatitude(rows_index):
    return jnp.pi * (rows_index.astype(jnp.float32) + 0.5) / GRID_LAT


def legendre(orders, cosine, sine_row, length):
    real_type = cosine.dtype
    order_real = orders.astype(real_type)
    ladder = jnp.arange(2, length + 1).astype(real_type)
    summands = jnp.where(
        ladder[None, :] <= order_real, jnp.log((2.0 * ladder + 1.0) / (2.0 * ladder))[None, :], 0.0
    )
    log_start = 0.5 * (
        jnp.where(order_real > 0.0, jnp.log(3.0), 0.0) + jnp.sum(summands, axis=1, keepdims=True)
    ) + order_real * jnp.log(sine_row)
    current = jnp.ones(log_start.shape, real_type)
    previous = jnp.zeros(log_start.shape, real_type)

    def recur(carried, degree):
        current, previous, log_scale = carried
        degree_real = degree.astype(real_type)
        active = degree_real > order_real
        raising = jnp.sqrt(
            jnp.maximum(4.0 * degree_real * degree_real - 1.0, 0.0)
            / jnp.maximum(degree_real * degree_real - order_real * order_real, 1.0)
        )
        lower_degree = degree_real - 1.0
        lowering = jnp.sqrt(
            jnp.maximum(lower_degree * lower_degree - order_real * order_real, 0.0)
            / jnp.maximum(4.0 * lower_degree * lower_degree - 1.0, 1.0)
        )
        latest = raising * (cosine * current - lowering * previous)
        current_next = jnp.where(active, latest, current)
        previous_next = jnp.where(active, current, previous)
        result = jnp.where(degree_real >= order_real, current_next * jnp.exp(log_scale), 0.0)
        magnitude = jnp.abs(current_next) + jnp.abs(previous_next)
        return (
            (current_next / magnitude, previous_next / magnitude, log_scale + jnp.log(magnitude)),
            result,
        )

    _, values = lax.scan(
        recur, (current, previous, log_start), jnp.arange(length, dtype=jnp.int32), unroll=8
    )
    return values


def fourier_tables(waves, columns):
    phase = waves[None, :] * columns[:, None] % GRID_LON
    angle = 2.0 * jnp.pi / GRID_LON * phase.astype(jnp.float32)
    cosines = jnp.cos(angle)
    sines = jnp.sin(angle)
    forward = (
        jnp.stack([cosines, sines], axis=-1).reshape(columns.shape[0], 2 * waves.shape[0])
        / GRID_LON
    )
    inverse = jnp.stack([cosines.T, sines.T], axis=1).reshape(2 * waves.shape[0], columns.shape[0])
    return (forward, inverse)


def local(elevation, velocity, wind_forcing, ocean_depth, wet_mask, love_factor, wavenumbers):
    members, band_height, sector_width = elevation.shape
    lat_devices = lax.axis_size("lat")
    lon_devices = lax.axis_size("lon")
    band_index = lax.axis_index("lat")
    sector = lax.axis_index("lon")
    sub_rows = band_height // lon_devices
    wave_total = wavenumbers.shape[0]
    wave_local = wave_total // lat_devices
    band_global = band_index * band_height + jnp.arange(band_height, dtype=jnp.int32)
    sine_band = jnp.sin(colatitude(band_global))
    rows_plus = band_index * band_height + jnp.arange(band_height + 2, dtype=jnp.int32) - 1
    sine_plus = jnp.sin(colatitude(rows_plus))
    rim_rows = band_index * band_height + jnp.arange(band_height + 4, dtype=jnp.int32) - 2
    inside = ((rim_rows >= 0) & (rim_rows < GRID_LAT)).astype(jnp.float32)[:, None]
    columns = sector * sector_width + jnp.arange(sector_width, dtype=jnp.int32)
    forward, inverse = fourier_tables(wavenumbers, columns)
    own_waves = lax.dynamic_slice_in_dim(wavenumbers, band_index * wave_local, wave_local)
    wave_rows = (
        jnp.arange(lat_devices, dtype=jnp.int32)[:, None] * band_height
        + sector * sub_rows
        + jnp.arange(sub_rows, dtype=jnp.int32)[None, :]
    ).reshape(-1)
    wave_angle = colatitude(wave_rows)
    wave_sine = jnp.sin(wave_angle)
    wave_weight = jnp.pi * wave_sine / (2.0 * GRID_LAT)
    tables = legendre(
        own_waves.reshape(wave_local, 1), jnp.cos(wave_angle)[None, :], wave_sine[None, :], DEGREES
    )
    love_weight = love_factor / (2.0 * jnp.arange(DEGREES).astype(jnp.float32) + 1.0)
    wet_float = wet_mask.astype(jnp.float32)
    wind_push = wind_forcing / ocean_depth[None]
    inverse_depth = 1.0 / ocean_depth
    statics = jnp.concatenate(
        [wind_push, inverse_depth[None], ocean_depth[None], wet_float[None]], axis=0
    )
    padded_static = with_halo(statics, (("lat", 1), ("lon", 2)), 2) * inside
    east_push = padded_static[0]
    south_push = padded_static[1]
    inverse_rim = padded_static[2]
    depth_rim = padded_static[3]
    wet_rim = padded_static[4]
    zonal_step = (step_ratio / sine_band)[:, None]
    meridional = 0.1 * GRID_LAT / GRID_LON
    rows_east = slice(2, band_height + 2)
    cols_east = slice(1, sector_width + 3)
    rows_south = slice(1, band_height + 3)
    cols_south = slice(2, sector_width + 2)
    load_mass = wet_float[None] * elevation
    partial_value = jnp.dot(
        load_mass.reshape(members * band_height, sector_width), forward, precision=highest
    ).reshape(members, band_height, 2 * wave_total)
    pending = lax.psum(partial_value, "lon")
    moved = lax.all_to_all(pending, "lat", split_axis=2, concat_axis=1, tiled=True)
    moved = moved.reshape(members, lat_devices, lon_devices, sub_rows, 2 * wave_local)
    moved = lax.dynamic_index_in_dim(moved, sector, 2, keepdims=False)
    moved = moved.reshape(members, lat_devices * sub_rows, 2 * wave_local)
    weighted = (
        moved.reshape(members, lat_devices * sub_rows, wave_local, 2)
        * wave_weight[None, :, None, None]
    )
    coeffs = jnp.einsum("ltr,ertc->etcl", tables, weighted, precision=highest)
    coeffs = lax.psum(coeffs, "lon")
    spectral = jnp.einsum("ltr,etcl->ertc", tables, coeffs * love_weight, precision=highest)
    spectral = spectral.reshape(members, lat_devices * sub_rows, 2 * wave_local)
    returned = lax.all_to_all(spectral, "lat", split_axis=1, concat_axis=2, tiled=True)
    segment = lax.all_gather(returned, "lon", axis=1, tiled=True)
    piece_rows = segment.shape[1]
    loading = jnp.dot(
        segment.reshape(members * piece_rows, 2 * wave_total), inverse, precision=highest
    ).reshape(members, piece_rows, sector_width)
    surface = elevation - loading
    stacked = jnp.concatenate([surface, velocity[:, 0], velocity[:, 1]], axis=0)
    padded = with_halo(stacked, (("lat", 1), ("lon", 2)), 2) * inside
    level = padded[:members]
    eastward = padded[members : 2 * members]
    southward = padded[2 * members :]
    east_now = eastward[:, rows_east, cols_east]
    south_here = southward[:, rows_east, cols_east]
    damping_east = (
        1.0
        + friction_rate
        * jnp.sqrt(east_now * east_now + south_here * south_here)
        * inverse_rim[rows_east, cols_east]
    )
    zonal_change = (
        level[:, 2 : band_height + 2, 2 : sector_width + 4]
        - level[:, 2 : band_height + 2, 0 : sector_width + 2]
    )
    east_next = (
        wet_rim[rows_east, cols_east]
        * (east_now + east_push[rows_east, cols_east] - zonal_step * zonal_change)
        / damping_east
    )
    east_here = eastward[:, rows_south, cols_south]
    south_now = southward[:, rows_south, cols_south]
    damping_south = (
        1.0
        + friction_rate
        * jnp.sqrt(east_here * east_here + south_now * south_now)
        * inverse_rim[rows_south, cols_south]
    )
    merid_change = (
        level[:, 2 : band_height + 4, 2 : sector_width + 2]
        - level[:, 0 : band_height + 2, 2 : sector_width + 2]
    )
    south_next = (
        wet_rim[rows_south, cols_south]
        * (south_now + south_push[rows_south, cols_south] - meridional * merid_change)
        / damping_south
    )
    east_flux = depth_rim[rows_east, cols_east] * east_next
    south_flux = sine_plus[:, None] * depth_rim[rows_south, cols_south] * south_next
    tendency = zonal_step * (east_flux[:, :, 2:] - east_flux[:, :, :-2]) + (meridional / sine_band)[
        :, None
    ] * (south_flux[:, 2:] - south_flux[:, :-2])
    elevation_next = elevation - wet_float[None] * tendency
    velocity_next = jnp.stack([east_next[:, :, 1:-1], south_next[:, 1:-1]], axis=1)
    return (elevation_next, velocity_next, loading)


def solution(mesh):
    return jax.shard_map(
        local,
        mesh=mesh,
        in_specs=(
            P(None, "lat", "lon"),
            P(None, None, "lat", "lon"),
            P(None, "lat", "lon"),
            P("lat", "lon"),
            P("lat", "lon"),
            P(),
            P(),
        ),
        out_specs=(P(None, "lat", "lon"), P(None, None, "lat", "lon"), P(None, "lat", "lon")),
        check_vma=False,
    )
```

profile of v0, /device:TPU:1, one launch (start us, length us, event | category | flops | bytes accessed | tf_op | source)
XLA Modules:
  0.0 1319.7 jit_solution(9577436853540227012)
XLA Ops:
  0.6 1.9 fusion.37
  3.6 0.7 convolution_bitcast_fusion.2
  4.4 28.7 %psum.14 = f32[1,48,128]{2,1,0:T(8,128)S(1)} all-reduce(f32[1,48,128]{2,1,0:T(8,128)S(1)} %convolution_bitcast_fusion.2), channel_id=1, replica_groups=mesh['lat'=64,'lon'=8] {'lon'}, use_global_device_ids=true, to_apply=%region_0.1 | all-reduce | flops 6144 | bytes 49152 | tf_op jit(solution)/shard_map/psum | solution.py:141
  33.1 0.7 copy.44
  33.8 13.7 %all-to-all-start = ((f32[1,48,128]{1,0,2:T(1,128)}), f32[1,48,128]{1,0,2:T(1,128)S(1)}, u32[]{:S(2)}, u32[]{:S(2)}) async-start(f32[1,48,128]{1,0,2:T(1,128)} %copy.44), calls=%async_computation | async-start | bytes 131072 | tf_op jit(solution)/shard_map/all_to_all | solution.py:142
  48.3 6.8 collective-permute-start
  55.1 6.6 collective-permute-start.1
  62.9 1.3 fusion.33
  65.8 1145.0 %while.20 = (s32[]{:T(128)}, f32[1,384]{1,0:T(1,128)S(1)}, f32[1,384]{1,0:T(1,128)S(1)}, f32[1,384]{1,0:T(1,128)S(1)}, f32[135,8,1,384]{3,2,1,0:T(1,128)}, /*ind...) while((s32[]{:T(128)}, f32[1,384]{1,0:T(1,128)S(1)}, ...), condition=%wide.region_3.4_spmd.clone, body=%wide.region_2.3_spmd.clone.sunk | while | flops 48162 | bytes 176693 | solution.py:70
  65.8 0.7 fusion.101
  74.3 0.7 fusion.101
  82.8 0.7 fusion.101
  91.3 0.7 fusion.101
  99.8 0.7 fusion.101
  108.3 0.7 fusion.101
  354.2 0.7 fusion.101
  456.0 0.7 fusion.101
  591.7 0.7 fusion.101
  752.8 0.7 fusion.101
  1117.5 0.7 fusion.101
  1211.2 0.8 slice_bitcast_fusion.15
  1212.1 4.5 pad_maximum_fusion
  1216.6 0.9 pad_maximum_fusion.3
  1217.5 1.3 pad_maximum_fusion.1
  1218.8 0.7 fusion.92
  1219.6 4.4 collective-permute-start.2
  1224.0 4.4 collective-permute-start.3
  1228.8 1.5 convolution_bitcast_fusion.1
  1230.3 16.9 %psum.15 = f32[1,1,2,1081]{3,2,1,0:T(2,128)S(1)} all-reduce(f32[1,1,2,1081]{3,2,1,0:T(2,128)S(1)} %convolution_bitcast_fusion.1), channel_id=1, replica_groups=mesh['lat'=64,'lon'=8] {'lon'}, use_global_device_ids=true, to_apply=%region_4.5 | all-reduce | flops 2162 | bytes 17296 | tf_op jit(solution)/shard_map/psum | solution.py:151
  1247.1 0.9 fusion.23
  1248.0 0.8 copy.53
  1248.9 10.8 all-to-all-start.1
  1259.8 1.5 copy.57
  1261.3 1.2 reshape.663
  1262.6 1.8 concatenate.30
  1264.3 9.0 all-to-all-done.1
  1273.3 1.0 copy.54
  1274.7 15.9 %all_gather.3 = f32[1,48,128]{2,0,1:T(1,128)S(1)} all-gather(f32[1,6,128]{2,0,1:T(1,128)S(1)} %copy.56), channel_id=1, replica_groups=mesh['lat'=64,'lon'=8] {'lon'}, dimensions={1}, use_global_device_ids=true | all-gather | bytes 27648 | tf_op jit(solution)/shard_map/all_gather | solution.py:155
  1290.6 2.2 fusion.94
  1292.8 3.8 collective-permute-start.4
  1296.6 9.6 collective-permute-start.5
  1306.4 0.8 collective-permute-done.5
  1307.4 1.9 collective-permute-start.6
  1309.3 3.2 collective-permute-start.7
  1312.7 3.4 collective-permute-done.7
  1317.3 0.7 fusion.51
  1318.0 0.8 pad_maximum_fusion.4
  1318.8 0.8 fusion.55
  (2228 shorter events, 249.9 us)
Async XLA Ops:
  2.6 1.0 copy-start.5
  2.6 1.0 copy-start.8
  3.1 44.4 %copy-start = (f32[48,1080]{1,0:T(8,128)S(1)}, f32[48,1080]{1,0:T(8,128)}, u32[]{:S(2)}) copy-start(f32[48,1080]{1,0:T(8,128)} %param.12) | copy-start | bytes 622084
  3.1 44.5 %copy-start.10 = (f32[2,48,1080]{2,1,0:T(8,128)S(1)}, f32[2,48,1080]{2,1,0:T(8,128)}, u32[]{:S(2)}) copy-start(f32[2,48,1080]{2,1,0:T(8,128)} %param.11) | copy-start | bytes 1244164
  33.8 28.0 %copy-start.13 = (s32[64]{0:T(128)S(1)}, s32[64]{0:T(128)}, u32[]{:S(2)}) copy-start(s32[64]{0:T(128)} %param.15) | copy-start | bytes 772
  33.8 1194.6 %all-to-all-start = ((f32[1,48,128]{1,0,2:T(1,128)}), f32[1,48,128]{1,0,2:T(1,128)S(1)}, u32[]{:S(2)}, u32[]{:S(2)}) async-start(f32[1,48,128]{1,0,2:T(1,128)} %copy.44), calls=%async_computation | async-start | bytes 131072 | tf_op jit(solution)/shard_map/all_to_all | solution.py:142
  47.5 0.7 copy-start.3
  47.6 0.7 copy-start.4
  48.3 1169.2 %collective-permute-start = (f32[5,2,1080]{2,1,0:T(2,128)S(1)}, f32[5,2,1080]{2,1,0:T(2,128)S(1)}, u32[]{:S(2)}, u32[]{:S(2)}) collective-permute-start(f32[5,2,1080]{2,1,0:T(2,128)S(1)} %get-tuple-element.310), channel_id=1, source_target_pairs={{0,8},{8,16},{16,24},{24,32},{32,40},{40,48},{48,56},{56,64},{64,7... | collective-permute-start | bytes 129608 | tf_op jit(solution)/shard_map/ppermute | solution.py:22
  55.1 1162.4 %collective-permute-start.1 = (f32[5,2,1080]{2,1,0:T(2,128)S(1)}, f32[5,2,1080]{2,1,0:T(2,128)}, u32[]{:S(2)}, u32[]{:S(2)}) collective-permute-start(f32[5,2,1080]{2,1,0:T(2,128)S(1)} %get-tuple-element.311), channel_id=1, source_target_pairs={{8,0},{16,8},{24,16},{32,24},{40,32},{48,40},{56,48},{64,56},{72,6... | collective-permute-start | bytes 129608 | tf_op jit(solution)/shard_map/ppermute | solution.py:25
  65.8 1145.4 %copy-start.12 = (f32[1081]{0:T(1024)S(1)}, f32[1081]{0:T(1024)}, u32[]{:S(2)}) copy-start(f32[1081]{0:T(1024)} %param.14) | copy-start | bytes 12976
  65.8 1145.4 %copy-start.11 = (f32[1,2,48,1080]{3,2,1,0:T(8,128)S(1)}, f32[1,2,48,1080]{3,2,1,0:T(8,128)}, u32[]{:S(2)}) copy-start(f32[1,2,48,1080]{3,2,1,0:T(8,128)} %param.10) | copy-start | bytes 1244164
  1219.6 43.0 %collective-permute-start.2 = (f32[5,52,2]{2,1,0:T(8,128)}, f32[5,52,2]{2,1,0:T(8,128)}, u32[]{:S(2)}, u32[]{:S(2)}) collective-permute-start(f32[5,52,2]{2,1,0:T(8,128)} %get-tuple-element.309), channel_id=1, source_target_pairs={{0,1},{1,2},{2,3},{3,4},{4,5},{5,6},{6,7},{7,0},{8,9},{9,10},{10,1... | collective-permute-start | bytes 6248 | tf_op jit(solution)/shard_map/ppermute | solution.py:22
  1224.0 38.6 %collective-permute-start.3 = (f32[5,52,2]{2,1,0:T(8,128)}, f32[5,52,2]{2,1,0:T(8,128)}, u32[]{:S(2)}, u32[]{:S(2)}) collective-permute-start(f32[5,52,2]{2,1,0:T(8,128)} %get-tuple-element.308), channel_id=1, source_target_pairs={{1,0},{2,1},{3,2},{4,3},{5,4},{6,5},{7,6},{0,7},{9,8},{10,9},{11,1... | collective-permute-start | bytes 6248 | tf_op jit(solution)/shard_map/ppermute | solution.py:25
  1248.9 24.5 %all-to-all-start.1 = ((f32[1,384,2]{2,0,1:T(1,128)}), f32[1,384,2]{2,0,1:T(1,128)}, u32[]{:S(2)}, u32[]{:S(2)}) async-start(f32[1,384,2]{2,0,1:T(1,128)} %copy.53), calls=%async_computation.1 | async-start | bytes 393216 | tf_op jit(solution)/shard_map/all_to_all | solution.py:154
  1262.6 28.0 %copy-start.6 = (f32[1,48,1080]{2,1,0:T(8,128)S(1)}, f32[1,48,1080]{2,1,0:T(8,128)}, u32[]{:S(2)}) copy-start(f32[1,48,1080]{2,1,0:T(8,128)} %param.9) | copy-start | bytes 622084
  1262.6 30.2 %copy-start.1 = (f32[1,48,1080]{2,1,0:T(8,128)S(1)}, f32[1,48,1080]{2,1,0:T(8,128)}, u32[]{:S(2)}) copy-start(f32[1,48,1080]{2,1,0:T(8,128)} %get-tuple-element.316) | copy-start | bytes 622084
  1262.6 30.2 %copy-start.2 = (f32[1,48,1080]{2,1,0:T(8,128)S(1)}, f32[1,48,1080]{2,1,0:T(8,128)}, u32[]{:S(2)}) copy-start(f32[1,48,1080]{2,1,0:T(8,128)} %get-tuple-element.317) | copy-start | bytes 622084
  1292.8 13.6 %collective-permute-start.4 = (f32[3,2,1080]{2,1,0:T(2,128)S(1)}, f32[3,2,1080]{2,1,0:T(2,128)S(1)}, u32[]{:S(2)}, u32[]{:S(2)}) collective-permute-start(f32[3,2,1080]{2,1,0:T(2,128)S(1)} %get-tuple-element.314), channel_id=1, source_target_pairs={{0,8},{8,16},{16,24},{24,32},{32,40},{40,48},{48,56},{56,64},{64,7... | collective-permute-start | bytes 77768 | tf_op jit(solution)/shard_map/ppermute | solution.py:22
  1296.6 10.6 collective-permute-start.5
  1307.4 5.3 collective-permute-start.6
  1309.3 6.8 collective-permute-start.7
  1317.3 1.6 copy-start.7
  1317.3 1.5 copy-start.9
where the time goes:
time: 1330 us; the launch traced here: 1320 us
  loops' own time  894 us (67%)
  local copies, waits for them, and re-layouts  220 us (17%)
  starting transfers between devices  65.3 us (5%)
  blocking collectives  61.6 us (5%)
  other arithmetic  57.9 us (4%)
    another operation x1, loops' own time, legendre(): lax.scan(recur, (current, previous, log_start), jnp.arange(length, dtype=...  894 us
    slice x136, local copies, waits for them, and re-layouts, legendre(): lax.scan(recur, (current, previous, log_start), jnp.arange(length, dtype=...  91.6 us
    dynamic_update_slice x135, local copies, waits for them, and re-layouts, legendre(): lax.scan(recur, (current, previous, log_start), jnp.arange(length, dtype=...  82.3 us
    cos x272, local copies, waits for them, and re-layouts, local(): jnp.cos(wave_angle)[None, :]  32.7 us
    while x945, other arithmetic  30.1 us
    psum x1, blocking collectives, local(): pending = lax.psum(partial_value, 'lon')  28.7 us
  transfers between devices with their start and end apart: 10, of which 3 were waited for; matrix products, arithmetic and copies ran while one was open for 21% of the time, Pallas kernels for 0%

commit v1 on v0

v1 whole, which is shorter than its diff:
```python
import functools
import math

import jax
import jax.numpy as jnp
from jax import lax
from jax.experimental import pallas as pl
from jax.experimental.pallas import tpu as pltpu
from jax.sharding import PartitionSpec as P

GRID_LAT = 3072
GRID_LON = 8640
DEGREES = 1081
STEP_RATIO = 0.05
FRICTION = 0.1

BAND = 48
SLOT = 64
PAIR = 8
F32 = jnp.float32
BF16 = jnp.bfloat16
MESH = pl.DeviceIdType.MESH


def iota(shape, dim):
    return lax.broadcasted_iota(jnp.int32, shape, dim)


def halves(x):
    high = x.astype(BF16)
    return high, (x - high.astype(F32)).astype(BF16)


def rows_dot(a, b):
    return lax.dot_general(a, b, (((1,), (0,)), ((), ())), preferred_element_type=F32)


def rows_dot_t(a, b):
    return lax.dot_general(a, b, (((1,), (1,)), ((), ())), preferred_element_type=F32)


def circle(phase, period):
    turns = jnp.floor(phase * (4.0 / period) + 0.5)
    t = (phase - turns * (period / 4.0)) * (2.0 * math.pi / period)
    t2 = t * t
    s = t * (1.0 + t2 * (-1.0 / 6 + t2 * (1.0 / 120 + t2 * (-1.0 / 5040 + t2 * (1.0 / 362880)))))
    c = 1.0 + t2 * (-0.5 + t2 * (1.0 / 24 + t2 * (-1.0 / 720 + t2 * (1.0 / 40320))))
    quarter = turns.astype(jnp.int32) & 3
    odd = (quarter & 1) == 1
    cosine = jnp.where(odd, s, c)
    sine = jnp.where(odd, c, s)
    cosine = jnp.where((quarter == 1) | (quarter == 2), -cosine, cosine)
    sine = jnp.where(quarter >= 2, -sine, sine)
    return cosine, sine


def spectral_kernel(
    bands, sectors, width, wide, length,
    elevation, velocity, wind, depth, mask, love, numbers,
    out_spec, out_th, out_tl, out_rows, out_cols, out_sine,
    fields, mask_v, x_pad, part, part_in, place_out, place_in, coef, coef_in,
    back_out, back_in, gather_in, row_msg, row_in, col_msg, col_in,
    amu, bee, dee, raw, table_h, table_l,
    load_sem, rs_send, rs_recv, a_send, a_recv, c_send, c_recv,
    s_send, s_recv, g_send, g_recv, h_send, h_recv,
):
    groups = bands // PAIR
    band = lax.axis_index("lat")
    sector = lax.axis_index("lon")
    south = band >= bands // 2
    north_band = jnp.where(south, bands - 1 - band, band)
    group = north_band // 4
    member = jnp.where(south, 7 - north_band % 4, north_band % 4)
    quarter = north_band % 4

    def band_of(g, p):
        n = g * 4 + jnp.where(p >= 4, 7 - p, p)
        return jnp.where(p >= 4, bands - 1 - n, n)

    loads = []
    sources = [
        (mask, mask_v), (elevation.at[0], fields.at[0]), (velocity.at[0, 0], fields.at[1]),
        (velocity.at[0, 1], fields.at[2]), (wind.at[0], fields.at[3]),
        (wind.at[1], fields.at[4]), (depth, fields.at[5]),
    ]
    for i, (src, dst) in enumerate(sources):
        copy = pltpu.make_async_copy(src, dst, load_sem.at[i])
        copy.start()
        loads.append(copy)

    above = ((band + bands - 1) % bands, sector)
    below = ((band + 1) % bands, sector)
    left = (band, (sector + sectors - 1) % sectors)
    right = (band, (sector + 1) % sectors)
    lon_peers = [(band, (sector + d) % sectors) for d in range(1, sectors)]
    group_peers = [(band_of(group, (member + d) % PAIR), sector) for d in range(1, PAIR)]
    wave_peers = [(band_of((group + d) % groups, member), sector) for d in range(1, groups)]
    peers = lon_peers + group_peers + wave_peers + [above, below, left, right]
    barrier = pltpu.get_barrier_semaphore()
    for peer in peers:
        pl.semaphore_signal(barrier, inc=1, device_id=peer, device_id_type=MESH)

    lane = iota((1, 128), 1)
    sub = iota((8, 128), 0)

    def zonal(s, carry):
        waves = jnp.zeros((8, 128), F32)
        for p in range(8):
            waves = jnp.where(sub == p, numbers[s * 8 + p].astype(F32), waves)
        at = pl.multiple_of(s * 16, 16)
        for tile in range(wide // 128):
            t = lane + tile * 128
            column = sector * width + jnp.where(t < width + 16, t, t - wide)
            cosine, sine = circle(waves * column.astype(F32), GRID_LON)
            high, low = halves(jnp.concatenate([cosine, sine], axis=0))
            out_th[pl.ds(at, 16), tile * 128 : tile * 128 + 128] = high
            out_tl[pl.ds(at, 16), tile * 128 : tile * 128 + 128] = low
        return carry

    lax.fori_loop(0, sectors, zonal, 0)

    x_pad[...] = jnp.zeros_like(x_pad)
    loads[0].wait()
    loads[1].wait()
    x_pad[8:56, 0:width] = fields[0] * mask_v[...].astype(F32)
    x_high, x_low = halves(x_pad[...])
    t_high = out_th[...]
    sums = (
        rows_dot_t(t_high, x_high) + rows_dot_t(t_high, x_low) + rows_dot_t(out_tl[...], x_high)
    )
    for s in range(sectors):
        part[s] = sums[16 * s : 16 * s + 16]

    pl.semaphore_wait(barrier, len(peers))
    sends = []

    def send(src, dst, send_sem, recv_sem, peer):
        copy = pltpu.make_async_remote_copy(
            src_ref=src, dst_ref=dst, send_sem=send_sem, recv_sem=recv_sem,
            device_id=peer, device_id_type=MESH,
        )
        copy.start()
        sends.append(copy)
        return copy

    rs = [
        send(part.at[(sector + d) % sectors], part_in.at[d], rs_send.at[d], rs_recv.at[d],
             lon_peers[d - 1])
        for d in range(1, sectors)
    ]

    for i in range(2, 7):
        loads[i].wait()
    wet = mask_v[...].astype(F32)
    row_msg[0, 0:2, :] = fields[0, 0:2, :]
    row_msg[1, 0:2, :] = fields[0, BAND - 2 : BAND, :]
    for slot, index in ((2, 1), (3, 2), (4, 4), (5, 5)):
        row_msg[0, slot : slot + 1, :] = fields[index, 0:1, :]
        row_msg[1, slot : slot + 1, :] = fields[index, BAND - 1 : BAND, :]
    row_msg[0, 6:7, :] = wet[0:1]
    row_msg[1, 6:7, :] = wet[BAND - 1 : BAND]
    for slot, index in ((0, 0), (1, 1), (2, 2), (3, 3), (4, 5)):
        col_msg[0, :, 2 * slot : 2 * slot + 2] = fields[index, :, 0:2]
        col_msg[1, :, 2 * slot : 2 * slot + 2] = fields[index, :, width - 2 : width]
    col_msg[0, :, 10:12] = wet[:, 0:2]
    col_msg[1, :, 10:12] = wet[:, width - 2 : width]
    rims = [
        send(row_msg.at[0], row_in.at[1], h_send.at[0], h_recv.at[0], above),
        send(row_msg.at[1], row_in.at[0], h_send.at[1], h_recv.at[1], below),
        send(col_msg.at[0], col_in.at[1], h_send.at[2], h_recv.at[2], left),
        send(col_msg.at[1], col_in.at[0], h_send.at[3], h_recv.at[3], right),
    ]

    order = numbers[sector * 8 + member].astype(F32)
    lam = iota((1, 256), 1)
    row = group * (4 * BAND) + (lam // SLOT) * BAND - 8 + lam % SLOT
    row_real = row.astype(F32) + 0.5
    cosine, sine = circle(row_real, 2 * GRID_LAT)
    sine = jnp.abs(sine)

    def coefficients(i, carry):
        base = pl.multiple_of(i * 16, 16)
        degree = (base + iota((16, 128), 0)).astype(F32)
        active = degree > order
        gap = jnp.where(active, degree * degree - order * order, 1.0)
        raising = jnp.sqrt((4.0 * degree * degree - 1.0) / gap)
        lower = degree - 1.0
        under = jnp.where(active, lower * lower - order * order, 0.0)
        over = jnp.where(active, 4.0 * lower * lower - 1.0, 1.0)
        lowering = jnp.sqrt(under / over)
        raising = jnp.where(active, raising, 0.0)
        amu[pl.ds(base, 16), 0:128] = raising * cosine[:, 0:128]
        amu[pl.ds(base, 16), 128:256] = raising * cosine[:, 128:256]
        bee[pl.ds(base, 16), :] = raising * lowering
        return carry

    lax.fori_loop(0, length // 16, coefficients, 0)
    first = min(128, length)
    dee[...] = jnp.where(iota((first, 128), 0).astype(F32) == order, 1.0, 0.0)

    ladder = (lane + 1).astype(F32)
    ratio = jnp.where(
        (lane >= 1) & (ladder <= order), jnp.log((2.0 * ladder + 1.0) / (2.0 * ladder)), 0.0
    )
    norm = jnp.sum(ratio, axis=1, keepdims=True) + jnp.where(order > 0.0, math.log(3.0), 0.0)
    log_scale = 0.5 * norm + order * jnp.log(sine)

    def block(inject, i, carry):
        current, previous, scale = carry
        base = pl.multiple_of(i * 16, 16)
        root = jnp.exp(0.5 * scale)
        for t in range(16):
            b = bee[pl.ds(base + t, 1), :]
            rest = jnp.concatenate([b, b], axis=1) * previous
            if inject:
                d = dee[pl.ds(base + t, 1), :]
                rest = rest - jnp.concatenate([d, d], axis=1)
            latest = amu[pl.ds(base + t, 1), :] * current - rest
            raw[t : t + 1, :] = latest
            current, previous = latest, current
        high, low = halves(raw[...] * root * root)
        table_h[pl.ds(base, 16), :] = high
        table_l[pl.ds(base, 16), :] = low
        large = jnp.maximum(jnp.abs(current), jnp.abs(previous)) > 2.0**20
        factor = jnp.where(large, 2.0**-40, 1.0)
        shift = jnp.where(large, 40.0 * math.log(2.0), 0.0)
        return current * factor, previous * factor, scale + shift

    zero = jnp.zeros((1, 256), F32)
    state = lax.fori_loop(
        0, first // 16, functools.partial(block, True), (zero, zero, log_scale)
    )

    for copy in rs:
        copy.wait_recv()
    total = part[sector]
    for d in range(1, sectors):
        total = total + part_in[d]
    slot_row = (band * BAND - 8 + iota((1, SLOT), 1)).astype(F32) + 0.5
    slot_row = jnp.minimum(slot_row, GRID_LAT - slot_row)
    slot_sine = circle(slot_row, 2 * GRID_LAT)[1]
    total = total * (slot_sine * (math.pi / (2.0 * GRID_LAT) / GRID_LON))
    from_row = iota((SLOT, 128), 0)
    to_row = iota((SLOT, 128), 1)
    target = jnp.where(south, SLOT - 1 - from_row, from_row) + SLOT * (quarter % 2)
    move = jnp.where(to_row == target, 1.0, 0.0).astype(BF16)
    high, low = halves(total)
    placed = rows_dot(high, move) + rows_dot(low, move)
    for p in range(PAIR):
        place_out[p, 0:1, :] = placed[p : p + 1]
        place_out[p, 1:2, :] = placed[8 + p : 9 + p]
    place_in[0] = place_out[member]
    moved = [
        send(place_out.at[(member + d) % PAIR], place_in.at[d], a_send.at[d], a_recv.at[d],
             group_peers[d - 1])
        for d in range(1, PAIR)
    ]

    lax.fori_loop(first // 16, length // 16, functools.partial(block, False), state)

    for copy in moved:
        copy.wait_recv()

    def piece(p):
        return place_in[(member + PAIR - p) % PAIR]

    north_rows = jnp.concatenate([piece(0) + piece(1), piece(2) + piece(3)], axis=1)
    south_rows = jnp.concatenate([piece(7) + piece(6), piece(5) + piece(4)], axis=1)
    both = jnp.concatenate([north_rows + south_rows, north_rows - south_rows], axis=0)
    high = both.astype(BF16).astype(F32)
    both = jnp.concatenate([high, both - high], axis=0).astype(BF16)
    product = rows_dot_t(both, table_h[...]) + rows_dot_t(both, table_l[...])
    product = product[0:4] + product[4:8]
    degree = iota((2, length), 1)
    even = (degree + numbers[sector * 8 + member]) % 2 == 0
    coef[...] = jnp.where(even, product[0:2], product[2:4])
    gathered = [
        send(coef, coef_in.at[d], c_send.at[d], c_recv.at[d], wave_peers[d - 1])
        for d in range(1, groups)
    ]
    for copy in gathered:
        copy.wait_recv()
    whole = coef[...]
    for d in range(1, groups):
        whole = whole + coef_in[d]
    whole = whole * (love[...] / (2.0 * iota((1, length), 1).astype(F32) + 1.0))
    split = jnp.concatenate([jnp.where(even, whole, 0.0), jnp.where(even, 0.0, whole)], axis=0)
    high = split.astype(BF16).astype(F32)
    split = jnp.concatenate([high, split - high], axis=0).astype(BF16)
    fields_back = rows_dot(split, table_h[...]) + rows_dot(split, table_l[...])
    fields_back = fields_back[0:4] + fields_back[4:8]
    north_back = fields_back[0:2] + fields_back[2:4]
    south_back = fields_back[0:2] - fields_back[2:4]
    for k in range(2):
        back_out[k] = north_back[:, 128 * k : 128 * k + 128]
        back_out[2 + k] = south_back[:, 128 * k : 128 * k + 128]

    def message(p):
        return jnp.where(p >= 4, 2 + (7 - p) // 2, p // 2)

    back_in[member] = back_out[message(member)]
    returned = []
    for d in range(1, PAIR):
        p = (member + d) % PAIR
        returned.append(
            send(back_out.at[message(p)], back_in.at[member], s_send.at[d], s_recv.at[d],
                 group_peers[d - 1])
        )
    for copy in returned:
        copy.wait_recv()
    gather_in[sector] = back_in[...]
    spread = [
        send(back_in, gather_in.at[sector], g_send.at[d], g_recv.at[d], lon_peers[d - 1])
        for d in range(1, sectors)
    ]

    sub_row = (band * BAND - 8 + iota((SLOT, 128), 0)).astype(F32) + 0.5
    sub_row = jnp.minimum(sub_row, GRID_LAT - sub_row)
    out_sine[...] = circle(sub_row, 2 * GRID_LAT)[1]
    for copy in rims:
        copy.wait_recv()
    out_rows[...] = row_in[...]
    out_cols[...] = col_in[...]
    for copy in spread:
        copy.wait_recv()
    for s in range(sectors):
        for p in range(PAIR):
            for c in range(2):
                at = 16 * s + 8 * c + p
                out_spec[at : at + 1, :] = gather_in[s, p, c : c + 1, :]
    for copy in sends:
        copy.wait_send()


def update_kernel(
    bands, width, wide,
    elevation, velocity, wind, depth, mask, spec, th, tl, rim_rows, rim_cols, sine,
    new_elevation, new_velocity, loading,
    padded, surface, south_flux, loads,
):
    band = lax.axis_index("lat")
    south = band >= bands // 2
    quarter = jnp.where(south, bands - 1 - band, band) % 4

    to_row = iota((SLOT, 128), 0)
    from_row = iota((SLOT, 128), 1)
    source = jnp.where(south, SLOT - 1 - to_row, to_row) + SLOT * (quarter % 2)
    move = jnp.where(from_row == source, 1.0, 0.0).astype(BF16)
    high, low = halves(spec[...])
    high = rows_dot_t(move, high).astype(BF16)
    low = rows_dot_t(move, low).astype(BF16)
    t_high = th[...]
    loads[...] = rows_dot(high, t_high) + rows_dot(low, t_high) + rows_dot(high, tl[...])

    body = slice(8, 8 + BAND)
    padded[0, body, 0:width] = elevation[0]
    padded[1, body, 0:width] = velocity[0, 0]
    padded[2, body, 0:width] = velocity[0, 1]
    padded[3, body, 0:width] = wind[0]
    padded[4, body, 0:width] = wind[1]
    padded[5, body, 0:width] = depth[...]
    padded[6, body, 0:width] = mask[...].astype(F32)
    padded[0, 6:8, 0:width] = rim_rows[0, 0:2, :]
    padded[0, 56:58, 0:width] = rim_rows[1, 0:2, :]
    for slot, index in ((2, 1), (3, 2), (4, 4), (5, 5), (6, 6)):
        padded[index, 7:8, 0:width] = rim_rows[0, slot : slot + 1, :]
        padded[index, 56:57, 0:width] = rim_rows[1, slot : slot + 1, :]
    for slot, index in ((0, 0), (1, 1), (2, 2), (3, 3), (4, 5), (5, 6)):
        padded[index, body, wide - 2 : wide] = rim_cols[0, :, 2 * slot : 2 * slot + 2]
        padded[index, body, width : width + 2] = rim_cols[1, :, 2 * slot : 2 * slot + 2]

    meridional = 0.1 * GRID_LAT / GRID_LON
    sub = iota((8, 1), 0)
    for r in range(8):
        at = slice(8 * r, 8 * r + 8)
        row = band * BAND - 8 + 8 * r + sub
        inside = (row >= 0) & (row < GRID_LAT)
        load = loads[at, :]
        surface[8 + 8 * r : 16 + 8 * r, :] = jnp.where(inside, padded[0, at, :] - load, 0.0)
        if 1 <= r <= 6:
            loading[0, 8 * r - 8 : 8 * r, :] = load[:, 0:width]
    for r in range(8):
        at = slice(8 * r, 8 * r + 8)
        row = band * BAND - 8 + 8 * r + sub
        inside = (row >= 0) & (row < GRID_LAT)
        u = padded[1, at, :]
        v = padded[2, at, :]
        deep = padded[5, at, :]
        inverse = 1.0 / deep
        damping = 1.0 + FRICTION * jnp.sqrt(u * u + v * v) * inverse
        change = surface[9 + 8 * r : 17 + 8 * r, :] - surface[7 + 8 * r : 15 + 8 * r, :]
        new_v = padded[6, at, :] * (v + padded[4, at, :] * inverse - meridional * change) / damping
        flux = sine[at, 0:1] * deep * new_v
        south_flux[at, :] = jnp.where(inside, flux, 0.0)
        if 1 <= r <= 6:
            new_velocity[0, 1, 8 * r - 8 : 8 * r, :] = new_v[:, 0:width]
    for r in range(1, 7):
        at = slice(8 * r, 8 * r + 8)
        u = padded[1, at, :]
        v = padded[2, at, :]
        deep = padded[5, at, :]
        wet = padded[6, at, :]
        inverse = 1.0 / deep
        damping = 1.0 + FRICTION * jnp.sqrt(u * u + v * v) * inverse
        here = surface[8 + 8 * r : 16 + 8 * r, :]
        change = pltpu.roll(here, wide - 1, 1) - pltpu.roll(here, 1, 1)
        row_sine = sine[at, 0:1]
        zonal = STEP_RATIO / row_sine
        new_u = wet * (u + padded[3, at, :] * inverse - zonal * change) / damping
        flux = deep * new_u
        east = pltpu.roll(flux, wide - 1, 1) - pltpu.roll(flux, 1, 1)
        down = south_flux[8 * r + 1 : 8 * r + 9, :] - south_flux[8 * r - 1 : 8 * r + 7, :]
        tendency = zonal * east + (meridional / row_sine) * down
        level = padded[0, at, :] - wet * tendency
        new_velocity[0, 0, 8 * r - 8 : 8 * r, :] = new_u[:, 0:width]
        new_elevation[0, 8 * r - 8 : 8 * r, :] = level[:, 0:width]


def local(bands, sectors, elevation, velocity, wind_forcing, ocean_depth, wet_mask, love_factor,
          wavenumbers):
    width = elevation.shape[2]
    wide = -(-(width + 18) // 128) * 128
    length = -(-DEGREES // 16) * 16
    groups = bands // PAIR
    love = jnp.pad(love_factor, (0, length - DEGREES)).reshape(1, length)
    vmem = pl.BlockSpec(memory_space=pltpu.VMEM)
    hbm = pl.BlockSpec(memory_space=pl.ANY)
    smem = pl.BlockSpec(memory_space=pltpu.SMEM)
    dma = pltpu.SemaphoreType.DMA
    spec, th, tl, rim_rows, rim_cols, sine = pl.pallas_call(
        functools.partial(spectral_kernel, bands, sectors, width, wide, length),
        out_shape=[
            jax.ShapeDtypeStruct((16 * sectors, 128), F32),
            jax.ShapeDtypeStruct((16 * sectors, wide), BF16),
            jax.ShapeDtypeStruct((16 * sectors, wide), BF16),
            jax.ShapeDtypeStruct((2, 8, width), F32),
            jax.ShapeDtypeStruct((2, BAND, 128), F32),
            jax.ShapeDtypeStruct((SLOT, 128), F32),
        ],
        in_specs=[hbm] * 5 + [vmem, smem],
        out_specs=[vmem] * 6,
        scratch_shapes=[
            pltpu.VMEM((6, BAND, width), F32),
            pltpu.VMEM((BAND, width), jnp.int32),
            pltpu.VMEM((SLOT, wide), F32),
            pltpu.VMEM((sectors, 16, SLOT), F32),
            pltpu.VMEM((sectors, 16, SLOT), F32),
            pltpu.VMEM((PAIR, 2, 128), F32),
            pltpu.VMEM((PAIR, 2, 128), F32),
            pltpu.VMEM((2, length), F32),
            pltpu.VMEM((groups, 2, length), F32),
            pltpu.VMEM((4, 2, 128), F32),
            pltpu.VMEM((PAIR, 2, 128), F32),
            pltpu.VMEM((sectors, PAIR, 2, 128), F32),
            pltpu.VMEM((2, 8, width), F32),
            pltpu.VMEM((2, 8, width), F32),
            pltpu.VMEM((2, BAND, 128), F32),
            pltpu.VMEM((2, BAND, 128), F32),
            pltpu.VMEM((length, 256), F32),
            pltpu.VMEM((length, 128), F32),
            pltpu.VMEM((min(128, length), 128), F32),
            pltpu.VMEM((16, 256), F32),
            pltpu.VMEM((length, 256), BF16),
            pltpu.VMEM((length, 256), BF16),
            dma((7,)),
            dma((sectors,)), dma((sectors,)),
            dma((PAIR,)), dma((PAIR,)),
            dma((groups,)), dma((groups,)),
            dma((PAIR,)), dma((PAIR,)),
            dma((sectors,)), dma((sectors,)),
            dma((4,)), dma((4,)),
        ],
        compiler_params=pltpu.CompilerParams(
            collective_id=0, has_side_effects=True, vmem_limit_bytes=24 * 1024 * 1024
        ),
        name="spectral",
    )(elevation, velocity, wind_forcing, ocean_depth, wet_mask, love, wavenumbers)
    return pl.pallas_call(
        functools.partial(update_kernel, bands, width, wide),
        out_shape=[
            jax.ShapeDtypeStruct(elevation.shape, F32),
            jax.ShapeDtypeStruct(velocity.shape, F32),
            jax.ShapeDtypeStruct(elevation.shape, F32),
        ],
        in_specs=[vmem] * 11,
        out_specs=[vmem] * 3,
        scratch_shapes=[
            pltpu.VMEM((7, SLOT, wide), F32),
            pltpu.VMEM((SLOT + 16, wide), F32),
            pltpu.VMEM((SLOT, wide), F32),
            pltpu.VMEM((SLOT, wide), F32),
        ],
        compiler_params=pltpu.CompilerParams(vmem_limit_bytes=24 * 1024 * 1024),
        name="update",
    )(elevation, velocity, wind_forcing, ocean_depth, wet_mask, spec, th, tl, rim_rows, rim_cols,
      sine)


def solution(mesh):
    bands, sectors = mesh.shape["lat"], mesh.shape["lon"]
    return jax.shard_map(
        functools.partial(local, bands, sectors),
        mesh=mesh,
        in_specs=(
            P(None, "lat", "lon"),
            P(None, None, "lat", "lon"),
            P(None, "lat", "lon"),
            P("lat", "lon"),
            P("lat", "lon"),
            P(),
            P(),
        ),
        out_specs=(P(None, "lat", "lon"), P(None, None, "lat", "lon"), P(None, "lat", "lon")),
        check_vma=False,
    )
```

time: 1330 us -> 59.3 us (0.04)
  loops' own time: 894 us -> 0 us
  local copies, waits for them, and re-layouts: 220 us -> 6.19 us
  starting transfers between devices: 65.3 us -> 0 us
  blocking collectives: 61.6 us -> 0 us
  other arithmetic: 57.9 us -> 0 us
  Pallas kernels: 0 us -> 52.1 us
    another operation x1 -> x0, loops' own time: 894 us -> none  [legendre(): lax.scan(recur, (current, previous, log_start), jnp.arange(length, dtype=...]
    slice x138 -> x0, local copies, waits for them, and re-layouts: 92.4 us -> none  [the longest x136 91.6 us: legendre(): lax.scan(recur, (current, previous, log_start), jnp.arange(length, dtype=...]
    dynamic_update_slice x135 -> x0, local copies, waits for them, and re-layouts: 82.3 us -> none  [legendre(): lax.scan(recur, (current, previous, log_start), jnp.arange(length, dtype=...]
    pallas_call x0 -> x2, Pallas kernels: none -> 52.1 us  [the longest x1 50.1 us: local(): pl.pallas_call(functools.partial(spectral_kernel, bands, sectors, width,...]
    psum x2 -> x0, blocking collectives: 45.6 us -> none  [the longest x1 28.7 us: local(): pending = lax.psum(partial_value, 'lon')]
    ppermute x8 -> x0, starting transfers between devices: 40.7 us -> none  [the longest x4 23.8 us: with_halo(): lax.ppermute(lax.slice_in_dim(block, 0, width, axis=dim), axis, backward)]
    cos x272 -> x0, local copies, waits for them, and re-layouts: 32.7 us -> none  [local(): jnp.cos(wave_angle)[None, :]]
    while x945 -> x0, other arithmetic: 30.1 us -> none
  transfers between devices with their start and end apart: 10 -> 0, of which waited for: 3 -> 0; matrix products, arithmetic and copies ran while one was open for 21% -> 0% of each run, Pallas kernels for 0% -> 0%
where the time goes in v1:
time: 59.3 us; the launch traced here: 58.9 us
  Pallas kernels  52.1 us (88%)
  local copies, waits for them, and re-layouts  6.19 us (10%)
  between operations  0.65 us (1%)
    pallas_call x1, Pallas kernels, local(): pl.pallas_call(functools.partial(spectral_kernel, bands, sectors, width,...  50.1 us
    unnamed x12, local copies, waits for them, and re-layouts  5.48 us
    pallas_call x1, Pallas kernels, local(): pl.pallas_call(functools.partial(update_kernel, bands, width, wide), out_...  1.99 us

profile of v1, /device:TPU:1, one launch (start us, length us, event | category | flops | bytes accessed | tf_op | source)
XLA Modules:
  0.0 58.9 jit_solution(15554372343336518621)
XLA Ops:
  0.6 0.7 %pad.4 = f32[1088]{0:T(1024)S(1)} pad(f32[1081]{0:T(1024)} %param.12, f32[]{:T(128)} %constant.2.clone.1), padding=0_7 | pad | bytes 8680 | tf_op jit(solution)/shard_map/jit(_pad)/pad | solution.py:425
  1.3 0.0 copy-start.5
  1.3 0.6 %copy-done.5 = s32[64]{0:T(128)S(1)} copy-done((s32[64]{0:T(128)S(1)}, s32[64]{0:T(128)}, u32[]{:S(2)}) %copy-start.5) | copy-done | bytes 280
  2.0 0.0 copy-start
  2.0 1.0 %copy-done = f32[1,2,48,1080]{3,2,1,0:T(8,128)S(1)} copy-done((f32[1,2,48,1080]{3,2,1,0:T(8,128)S(1)}, f32[1,2,48,1080]{3,2,1,0:T(8,128)}, u32[]{:S(2)}) %copy-start) | copy-done | bytes 414744
  3.0 0.0 copy-start.1
  3.0 1.0 %copy-done.1 = f32[2,48,1080]{2,1,0:T(8,128)S(1)} copy-done((f32[2,48,1080]{2,1,0:T(8,128)S(1)}, f32[2,48,1080]{2,1,0:T(8,128)}, u32[]{:S(2)}) %copy-start.1) | copy-done | bytes 414744
  4.0 0.0 copy-start.2
  4.0 0.9 %copy-done.2 = f32[1,48,1080]{2,1,0:T(8,128)S(1)} copy-done((f32[1,48,1080]{2,1,0:T(8,128)S(1)}, f32[1,48,1080]{2,1,0:T(8,128)}, u32[]{:S(2)}) %copy-start.2) | copy-done | bytes 207384
  5.0 0.0 copy-start.3
  5.0 0.9 %copy-done.3 = f32[48,1080]{1,0:T(8,128)S(1)} copy-done((f32[48,1080]{1,0:T(8,128)S(1)}, f32[48,1080]{1,0:T(8,128)}, u32[]{:S(2)}) %copy-start.3) | copy-done | bytes 207384
  5.9 0.0 copy-start.4
  5.9 0.9 %copy-done.4 = s32[48,1080]{1,0:T(8,128)S(1)} copy-done((s32[48,1080]{1,0:T(8,128)S(1)}, s32[48,1080]{1,0:T(8,128)}, u32[]{:S(2)}) %copy-start.4) | copy-done | bytes 207384
  6.8 50.1 %spectral.1 = (f32[128,128]{1,0:T(8,128)S(1)}, bf16[128,1152]{1,0:T(8,128)(2,1)S(1)}, bf16[128,1152]{1,0:T(8,128)(2,1)S(1)}, f32[2,8,1080]{2,1,0:T(8,128)S(1)}, ...) custom-call(f32[1,48,1080]{2,1,0:T(8,128)S(1)} %copy-done.2, f32[1,2,48,1080]{3,2,1,0:T(8,128)S(1)} %copy-done, ...), custom_call_target="tpu_custom_call" | custom-call | tf_op jit(solution)/shard_map/spectral/pallas_call | solution.py:430
  56.9 2.0 %update.1 = (f32[1,48,1080]{2,1,0:T(8,128)}, f32[1,2,48,1080]{3,2,1,0:T(8,128)}, f32[1,48,1080]{2,1,0:T(8,128)}) custom-call(f32[1,48,1080]{2,1,0:T(8,128)S(1)} %copy-done.2, f32[1,2,48,1080]{3,2,1,0:T(8,128)S(1)} %copy-done, f32[2,48,1080]{2,1,0:T(8,128)S(1)} %copy-done.1, f32[48,1080]{1,0:T(8,128)S(1)} %copy-done.3, s32[48,1080]{1,0:T(8,128)S(1)} %copy-done.4, ...), custom_call_target="tpu_custom_call" | custom-call | tf_op jit(solution)/shard_map/update/pallas_call | solution.py:478
  (1 shorter events, 0.0 us)
Async XLA Ops:
  1.3 0.7 %copy-start.5 = (s32[64]{0:T(128)S(1)}, s32[64]{0:T(128)}, u32[]{:S(2)}) copy-start(s32[64]{0:T(128)} %numbers.1) | copy-start | bytes 772
  2.0 1.0 %copy-start = (f32[1,2,48,1080]{3,2,1,0:T(8,128)S(1)}, f32[1,2,48,1080]{3,2,1,0:T(8,128)}, u32[]{:S(2)}) copy-start(f32[1,2,48,1080]{3,2,1,0:T(8,128)} %velocity.3) | copy-start | bytes 1244164
  3.0 1.0 %copy-start.1 = (f32[2,48,1080]{2,1,0:T(8,128)S(1)}, f32[2,48,1080]{2,1,0:T(8,128)}, u32[]{:S(2)}) copy-start(f32[2,48,1080]{2,1,0:T(8,128)} %wind.3) | copy-start | bytes 1244164
  4.0 0.9 %copy-start.2 = (f32[1,48,1080]{2,1,0:T(8,128)S(1)}, f32[1,48,1080]{2,1,0:T(8,128)}, u32[]{:S(2)}) copy-start(f32[1,48,1080]{2,1,0:T(8,128)} %elevation.3) | copy-start | bytes 622084
  5.0 0.9 %copy-start.3 = (f32[48,1080]{1,0:T(8,128)S(1)}, f32[48,1080]{1,0:T(8,128)}, u32[]{:S(2)}) copy-start(f32[48,1080]{1,0:T(8,128)} %depth.3) | copy-start | bytes 622084
  5.9 0.9 %copy-start.4 = (s32[48,1080]{1,0:T(8,128)S(1)}, s32[48,1080]{1,0:T(8,128)}, u32[]{:S(2)}) copy-start(s32[48,1080]{1,0:T(8,128)} %mask.3) | copy-start | bytes 622084

commit v2 on v1

v2 whole, which is shorter than its diff:
```python
import functools
import math

import jax
import jax.numpy as jnp
from jax import lax
from jax.experimental import pallas as pl
from jax.experimental.pallas import tpu as pltpu
from jax.sharding import PartitionSpec as P

GRID_LAT = 3072
GRID_LON = 8640
DEGREES = 1081
STEP_RATIO = 0.05
FRICTION = 0.1

BAND = 48
SLOT = 64
PILE = 8
F32 = jnp.float32
BF16 = jnp.bfloat16
MESH = pl.DeviceIdType.MESH
HBM = pltpu.MemorySpace.HBM
SPLIT = 44


def iota(shape, dim):
    return lax.broadcasted_iota(jnp.int32, shape, dim)


def halves(x):
    high = x.astype(BF16)
    return high, (x - high.astype(F32)).astype(BF16)


def rows_dot(a, b):
    return lax.dot_general(a, b, (((1,), (0,)), ((), ())), preferred_element_type=F32)


def rows_dot_t(a, b):
    return lax.dot_general(a, b, (((1,), (1,)), ((), ())), preferred_element_type=F32)


def circle(phase, period):
    turns = jnp.floor(phase * (4.0 / period) + 0.5)
    t = (phase - turns * (period / 4.0)) * (2.0 * math.pi / period)
    t2 = t * t
    s = t * (1.0 + t2 * (-1.0 / 6 + t2 * (1.0 / 120 + t2 * (-1.0 / 5040 + t2 * (1.0 / 362880)))))
    c = 1.0 + t2 * (-0.5 + t2 * (1.0 / 24 + t2 * (-1.0 / 720 + t2 * (1.0 / 40320))))
    quarter = turns.astype(jnp.int32) & 3
    odd = (quarter & 1) == 1
    cosine = jnp.where(odd, s, c)
    sine = jnp.where(odd, c, s)
    cosine = jnp.where((quarter == 1) | (quarter == 2), -cosine, cosine)
    sine = jnp.where(quarter >= 2, -sine, sine)
    return cosine, sine


def spectral_kernel(
    bands, sectors, width, wide, length,
    elevation, velocity, wind, depth, mask, love, waves_hbm,
    out_spec, out_th, out_tl, out_fields, out_sine,
    numbers, fields, mask_v, love_v, x_pad, part, part_in, place_out, place_in, coef, coef_in,
    back_out, back_in, ring_out, row_msg, row_in, col_msg, col_in,
    ladder_v, ladder_s, raw, table_h, table_l, spec_in,
    load_sem, rs_send, rs_recv, a_send, a_recv, c_send, c_recv,
    s_send, s_recv, g_send, g_recv, h_send, h_recv,
):
    depths = bands // PILE
    ring = 2 * sectors
    band = lax.axis_index("lat")
    sector = lax.axis_index("lon")
    z, x, half = band // 8, (band // 2) % 4, band % 2
    place = half * sectors + sector

    sources = [
        (waves_hbm, numbers), (mask, mask_v), (elevation.at[0], fields.at[0]), (love, love_v),
        (velocity.at[0, 0], fields.at[1]), (velocity.at[0, 1], fields.at[2]),
        (wind.at[0], fields.at[3]), (wind.at[1], fields.at[4]), (depth, fields.at[5]),
    ]
    loads = [pltpu.make_async_copy(a, b, load_sem.at[i]) for i, (a, b) in enumerate(sources)]
    for copy in loads:
        copy.start()

    above = ((band + bands - 1) % bands, sector)
    below = ((band + 1) % bands, sector)
    left = (band, (sector + sectors - 1) % sectors)
    right = (band, (sector + 1) % sectors)

    def ring_peer(t):
        return (z * 8 + x * 2 + t // sectors, t % sectors)

    ring_peers = [ring_peer((place + d) % ring) for d in range(1, ring)]
    x_peers = [(z * 8 + ((x + d) % 4) * 2 + half, sector) for d in range(1, 4)]
    z_peers = [(((z + d) % depths) * 8 + x * 2 + half, sector) for d in range(1, depths)]
    peers = ring_peers + x_peers + z_peers + [above, below, left, right]
    barrier = pltpu.get_barrier_semaphore()
    for peer in peers:
        pl.semaphore_signal(barrier, inc=1, device_id=peer, device_id_type=MESH)

    loads[0].wait()

    lane = iota((1, 128), 1)
    sub = iota((8, 128), 0)

    def zonal(s, carry):
        waves = jnp.zeros((8, 128), F32)
        for p in range(8):
            waves = jnp.where(sub == p, numbers[s * 8 + p].astype(F32), waves)
        at = pl.multiple_of(s * 16, 16)
        for tile in range(wide // 128):
            t = lane + tile * 128
            column = sector * width + jnp.where(t < width + 16, t, t - wide)
            cosine, sine = circle(waves * column.astype(F32), GRID_LON)
            high, low = halves(
                jnp.concatenate([cosine[0:4], sine[0:4], cosine[4:8], sine[4:8]], axis=0)
            )
            out_th[pl.ds(at, 16), tile * 128 : tile * 128 + 128] = high
            out_tl[pl.ds(at, 16), tile * 128 : tile * 128 + 128] = low
        return carry

    lax.fori_loop(0, sectors, zonal, 0)

    x_pad[...] = jnp.zeros_like(x_pad)
    loads[1].wait()
    loads[2].wait()
    x_pad[8:56, 0:width] = fields[0] * mask_v[...].astype(F32)
    x_high, x_low = halves(x_pad[...])
    t_high = out_th[...]
    sums = (
        rows_dot_t(t_high, x_high) + rows_dot_t(t_high, x_low) + rows_dot_t(out_tl[...], x_high)
    )
    for t in range(ring):
        part[t] = sums[8 * t : 8 * t + 8]

    number = numbers[place * 4 + x]
    order = number.astype(F32)
    degree = (iota((16, 128), 0) * 128 + iota((16, 128), 1)).astype(F32)
    active = degree > order
    gap = jnp.where(active, degree * degree - order * order, 1.0)
    raising = jnp.sqrt((4.0 * degree * degree - 1.0) / gap)
    lower = degree - 1.0
    under = jnp.where(active, lower * lower - order * order, 0.0)
    over = jnp.where(active, 4.0 * lower * lower - 1.0, 1.0)
    raising = jnp.where(active, raising, 0.0)
    ladder_v[0:16, :] = raising
    ladder_v[16:32, :] = raising * jnp.sqrt(under / over)
    to_scalar = pltpu.make_async_copy(ladder_v, ladder_s, load_sem.at[len(sources)])
    to_scalar.start()

    pl.semaphore_wait(barrier, len(peers))
    sends = []

    def send(src, dst, send_sem, recv_sem, peer):
        copy = pltpu.make_async_remote_copy(
            src_ref=src, dst_ref=dst, send_sem=send_sem, recv_sem=recv_sem,
            device_id=peer, device_id_type=MESH,
        )
        copy.start()
        sends.append(copy)
        return copy

    rs = [
        send(part.at[(place + d) % ring], part_in.at[place], rs_send.at[d], rs_recv.at[d],
             ring_peers[d - 1])
        for d in range(1, ring)
    ]
    part_in[place] = part[place]

    for i in range(3, len(sources)):
        loads[i].wait()
    wet = mask_v[...].astype(F32)
    row_msg[0, 0:2, :] = fields[0, 0:2, :]
    row_msg[1, 0:2, :] = fields[0, BAND - 2 : BAND, :]
    for slot, index in ((2, 1), (3, 2), (4, 4), (5, 5)):
        row_msg[0, slot : slot + 1, :] = fields[index, 0:1, :]
        row_msg[1, slot : slot + 1, :] = fields[index, BAND - 1 : BAND, :]
    row_msg[0, 6:7, :] = wet[0:1]
    row_msg[1, 6:7, :] = wet[BAND - 1 : BAND]
    for slot, index in ((0, 0), (1, 1), (2, 2), (3, 3), (4, 5)):
        col_msg[0, :, 2 * slot : 2 * slot + 2] = fields[index, :, 0:2]
        col_msg[1, :, 2 * slot : 2 * slot + 2] = fields[index, :, width - 2 : width]
    col_msg[0, :, 10:12] = wet[:, 0:2]
    col_msg[1, :, 10:12] = wet[:, width - 2 : width]
    rims = [
        send(row_msg.at[0], row_in.at[1], h_send.at[0], h_recv.at[0], above),
        send(row_msg.at[1], row_in.at[0], h_send.at[1], h_recv.at[1], below),
        send(col_msg.at[0], col_in.at[1], h_send.at[2], h_recv.at[2], left),
        send(col_msg.at[1], col_in.at[0], h_send.at[3], h_recv.at[3], right),
    ]

    row = (z * 8 + 2 * iota((4, 128), 0) + iota((4, 128), 1) // SLOT) * BAND - 8
    row = row + iota((4, 128), 1) % SLOT
    cosine, sine = circle(row.astype(F32) + 0.5, 2 * GRID_LAT)
    ladder = (lane + 1).astype(F32)
    ratio = jnp.where(
        (lane >= 1) & (ladder <= order), jnp.log((2.0 * ladder + 1.0) / (2.0 * ladder)), 0.0
    )
    norm = jnp.sum(ratio, axis=1, keepdims=True) + jnp.where(order > 0.0, math.log(3.0), 0.0)
    log_scale = 0.5 * norm + order * jnp.log(jnp.abs(sine))
    to_scalar.wait()

    def block(inject, i, carry):
        current, previous, scale = carry
        base = pl.multiple_of(i * 16, 16)
        line, first = i // 8, (i % 8) * 16
        root = jnp.exp(0.5 * scale)
        for t in range(16):
            rest = ladder_s[16 + line, first + t] * previous
            if inject:
                rest = rest - jnp.where(base + t == number, 1.0, 0.0)
            latest = (ladder_s[line, first + t] * cosine) * current - rest
            raw[4 * t : 4 * t + 4, :] = latest
            current, previous = latest, current
        for k in range(4):
            factor = root[k : k + 1]
            high, low = halves(raw[pl.ds(k, 16, stride=4), :] * factor * factor)
            table_h[pl.ds(base, 16), 128 * k : 128 * k + 128] = high
            table_l[pl.ds(base, 16), 128 * k : 128 * k + 128] = low
        large = jnp.maximum(jnp.abs(current), jnp.abs(previous)) > 2.0**20
        factor = jnp.where(large, 2.0**-40, 1.0)
        shift = jnp.where(large, 40.0 * math.log(2.0), 0.0)
        return current * factor, previous * factor, scale + shift

    zero = jnp.zeros((4, 128), F32)
    blocks = length // 16
    early = min(8, blocks)
    middle = min(SPLIT, blocks)
    state = (zero, zero, log_scale)
    state = lax.fori_loop(0, early, functools.partial(block, True), state)
    state = lax.fori_loop(early, middle, functools.partial(block, False), state)

    for copy in rs:
        copy.wait_recv()
    pieces = []
    for h in range(2):
        total = part_in[h * sectors]
        for s in range(1, sectors):
            total = total + part_in[h * sectors + s]
        pieces.append(total)
    total = jnp.concatenate(pieces, axis=1)
    slot_row = (z * 8 + x * 2 + lane // SLOT) * BAND - 8 + lane % SLOT
    slot_sine = circle(slot_row.astype(F32) + 0.5, 2 * GRID_LAT)[1]
    total = total * (slot_sine * (math.pi / (2.0 * GRID_LAT) / GRID_LON))
    for p in range(4):
        place_out[p, 0:1, :] = total[p : p + 1]
        place_out[p, 1:2, :] = total[4 + p : 5 + p]
    moved = [
        send(place_out.at[(x + d) % 4], place_in.at[x], a_send.at[d], a_recv.at[d],
             x_peers[d - 1])
        for d in range(1, 4)
    ]
    place_in[x] = place_out[x]

    lax.fori_loop(middle, blocks, functools.partial(block, False), state)

    for copy in moved:
        copy.wait_recv()
    rows = jnp.concatenate([place_in[k] for k in range(4)], axis=1)
    high = rows.astype(BF16).astype(F32)
    rows = jnp.concatenate([high, rows - high], axis=0).astype(BF16)
    product = rows_dot_t(rows, table_h[...]) + rows_dot_t(rows, table_l[...])
    coef[...] = product[0:2] + product[2:4]
    gathered = [
        send(coef, coef_in.at[d], c_send.at[d], c_recv.at[d], z_peers[d - 1])
        for d in range(1, depths)
    ]

    for copy in rims:
        copy.wait_recv()
    sub_row = band * BAND - 8 + iota((SLOT, 128), 0)
    band_sine = circle(sub_row.astype(F32) + 0.5, 2 * GRID_LAT)[1]
    out_sine[...] = band_sine
    body = slice(8, 8 + BAND)
    for index in range(6):
        out_fields[index, body, 0:width] = fields[index]
    out_fields[6, body, 0:width] = wet
    out_fields[0, 6:8, 0:width] = row_in[0, 0:2, :]
    out_fields[0, 56:58, 0:width] = row_in[1, 0:2, :]
    for slot, index in ((2, 1), (3, 2), (4, 4), (5, 5), (6, 6)):
        out_fields[index, 7:8, 0:width] = row_in[0, slot : slot + 1, :]
        out_fields[index, 56:57, 0:width] = row_in[1, slot : slot + 1, :]
    for slot, index in ((0, 0), (1, 1), (2, 2), (3, 3), (4, 5), (5, 6)):
        out_fields[index, body, wide - 2 : wide] = col_in[0, :, 2 * slot : 2 * slot + 2]
        out_fields[index, body, width : width + 2] = col_in[1, :, 2 * slot : 2 * slot + 2]
    meridional = 0.1 * GRID_LAT / GRID_LON

    def prepare(r, carry):
        at = pl.ds(pl.multiple_of(8 * r, 8), 8)
        u = out_fields[1, at, :]
        v = out_fields[2, at, :]
        inverse = 1.0 / out_fields[5, at, :]
        damping = 1.0 + FRICTION * jnp.sqrt(u * u + v * v) * inverse
        share = out_fields[6, at, :] / damping
        zonal_step = STEP_RATIO / out_sine[at, 0:1]
        out_fields[1, at, :] = share * (u + out_fields[3, at, :] * inverse)
        out_fields[2, at, :] = share * zonal_step
        out_fields[3, at, :] = share * (v + out_fields[4, at, :] * inverse)
        out_fields[4, at, :] = share * meridional
        return carry

    lax.fori_loop(0, SLOT // 8, prepare, 0)

    for copy in gathered:
        copy.wait_recv()
    whole = coef[...]
    for d in range(1, depths):
        whole = whole + coef_in[d]
    degrees = love_v.shape[1]
    weight = love_v[...] / (2.0 * iota((1, degrees), 1).astype(F32) + 1.0)
    weight = jnp.concatenate([weight, jnp.zeros((1, length - degrees), F32)], axis=1)
    whole = whole * weight
    high = whole.astype(BF16).astype(F32)
    whole = jnp.concatenate([high, whole - high], axis=0).astype(BF16)
    product = rows_dot(whole, table_h[...]) + rows_dot(whole, table_l[...])
    product = product[0:2] + product[2:4]
    for k in range(4):
        back_out[k] = product[:, 128 * k : 128 * k + 128]
    returned = [
        send(back_out.at[(x + d) % 4], back_in.at[x], s_send.at[d], s_recv.at[d], x_peers[d - 1])
        for d in range(1, 4)
    ]
    back_in[x] = back_out[x]
    for copy in returned:
        copy.wait_recv()
    for k in range(4):
        ring_out[k : k + 1, :] = back_in[k, 0:1, :]
        ring_out[4 + k : 5 + k, :] = back_in[k, 1:2, :]
    spread = [
        send(ring_out, spec_in.at[place], g_send.at[d], g_recv.at[d], ring_peers[d - 1])
        for d in range(1, ring)
    ]
    spec_in[place] = ring_out[...]
    for copy in spread:
        copy.wait_recv()
    out_spec[...] = spec_in[...]
    for copy in sends:
        copy.wait_send()


def update_kernel(
    bands, width, wide,
    spec, th, tl, fields, sine,
    new_elevation, new_velocity, loading,
    surface, south_flux, loads,
):
    band = lax.axis_index("lat")

    source = iota((SLOT, 128), 0) + SLOT * (band % 2)
    move = jnp.where(iota((SLOT, 128), 1) == source, 1.0, 0.0).astype(BF16)
    high, low = halves(spec[...].reshape(th.shape[0], 128))
    high = rows_dot_t(move, high).astype(BF16)
    low = rows_dot_t(move, low).astype(BF16)
    t_high = th[...]
    loads[...] = rows_dot(high, t_high) + rows_dot(low, t_high) + rows_dot(high, tl[...])

    meridional = 0.1 * GRID_LAT / GRID_LON
    sub = iota((8, 1), 0)
    for r in range(8):
        at = slice(8 * r, 8 * r + 8)
        row = band * BAND - 8 + 8 * r + sub
        inside = (row >= 0) & (row < GRID_LAT)
        load = loads[at, :]
        surface[8 + 8 * r : 16 + 8 * r, :] = jnp.where(inside, fields[0, at, :] - load, 0.0)
        if 1 <= r <= 6:
            loading[0, 8 * r - 8 : 8 * r, :] = load[:, 0:width]
    for r in range(8):
        at = slice(8 * r, 8 * r + 8)
        row = band * BAND - 8 + 8 * r + sub
        inside = (row >= 0) & (row < GRID_LAT)
        change = surface[9 + 8 * r : 17 + 8 * r, :] - surface[7 + 8 * r : 15 + 8 * r, :]
        new_v = fields[3, at, :] - fields[4, at, :] * change
        flux = sine[at, 0:1] * fields[5, at, :] * new_v
        south_flux[at, :] = jnp.where(inside, flux, 0.0)
        if 1 <= r <= 6:
            new_velocity[0, 1, 8 * r - 8 : 8 * r, :] = new_v[:, 0:width]
    for r in range(1, 7):
        at = slice(8 * r, 8 * r + 8)
        here = surface[8 + 8 * r : 16 + 8 * r, :]
        change = pltpu.roll(here, wide - 1, 1) - pltpu.roll(here, 1, 1)
        new_u = fields[1, at, :] - fields[2, at, :] * change
        flux = fields[5, at, :] * new_u
        east = pltpu.roll(flux, wide - 1, 1) - pltpu.roll(flux, 1, 1)
        down = south_flux[8 * r + 1 : 8 * r + 9, :] - south_flux[8 * r - 1 : 8 * r + 7, :]
        row_sine = sine[at, 0:1]
        tendency = (STEP_RATIO / row_sine) * east + (meridional / row_sine) * down
        level = fields[0, at, :] - fields[6, at, :] * tendency
        new_velocity[0, 0, 8 * r - 8 : 8 * r, :] = new_u[:, 0:width]
        new_elevation[0, 8 * r - 8 : 8 * r, :] = level[:, 0:width]


def local(bands, sectors, elevation, velocity, wind_forcing, ocean_depth, wet_mask, love_factor,
          wavenumbers):
    width = elevation.shape[2]
    wide = -(-(width + 18) // 128) * 128
    length = -(-DEGREES // 16) * 16
    depths = bands // PILE
    ring = 2 * sectors
    vmem = pl.BlockSpec(memory_space=pltpu.VMEM)
    hbm = pl.BlockSpec(memory_space=HBM)
    dma = pltpu.SemaphoreType.DMA
    shared = pl.pallas_call(
        functools.partial(spectral_kernel, bands, sectors, width, wide, length),
        out_shape=[
            jax.ShapeDtypeStruct((ring, 8, 128), F32),
            jax.ShapeDtypeStruct((8 * ring, wide), BF16),
            jax.ShapeDtypeStruct((8 * ring, wide), BF16),
            jax.ShapeDtypeStruct((7, SLOT, wide), F32),
            jax.ShapeDtypeStruct((SLOT, 128), F32),
        ],
        in_specs=[hbm] * 7,
        out_specs=[vmem] * 5,
        scratch_shapes=[
            pltpu.SMEM((8 * sectors,), jnp.int32),
            pltpu.VMEM((6, BAND, width), F32),
            pltpu.VMEM((BAND, width), jnp.int32),
            pltpu.VMEM((1, DEGREES), F32),
            pltpu.VMEM((SLOT, wide), F32),
            pltpu.VMEM((ring, 8, SLOT), F32),
            pltpu.VMEM((ring, 8, SLOT), F32),
            pltpu.VMEM((4, 2, 128), F32),
            pltpu.VMEM((4, 2, 128), F32),
            pltpu.VMEM((2, length), F32),
            pltpu.VMEM((depths, 2, length), F32),
            pltpu.VMEM((4, 2, 128), F32),
            pltpu.VMEM((4, 2, 128), F32),
            pltpu.VMEM((8, 128), F32),
            pltpu.VMEM((2, 8, width), F32),
            pltpu.VMEM((2, 8, width), F32),
            pltpu.VMEM((2, BAND, 128), F32),
            pltpu.VMEM((2, BAND, 128), F32),
            pltpu.VMEM((32, 128), F32),
            pltpu.SMEM((32, 128), F32),
            pltpu.VMEM((64, 128), F32),
            pltpu.VMEM((length, 512), BF16),
            pltpu.VMEM((length, 512), BF16),
            pltpu.VMEM((ring, 8, 128), F32),
            dma((10,)),
            dma((ring,)), dma((ring,)),
            dma((4,)), dma((4,)),
            dma((depths,)), dma((depths,)),
            dma((4,)), dma((4,)),
            dma((ring,)), dma((ring,)),
            dma((4,)), dma((4,)),
        ],
        compiler_params=pltpu.CompilerParams(
            collective_id=0, has_side_effects=True, vmem_limit_bytes=24 * 1024 * 1024
        ),
        name="spectral",
    )(*[
        pltpu.with_memory_space_constraint(array, HBM)
        for array in (elevation, velocity, wind_forcing, ocean_depth, wet_mask,
                      love_factor.reshape(1, DEGREES), wavenumbers)
    ])
    return pl.pallas_call(
        functools.partial(update_kernel, bands, width, wide),
        out_shape=[
            jax.ShapeDtypeStruct(elevation.shape, F32),
            jax.ShapeDtypeStruct(velocity.shape, F32),
            jax.ShapeDtypeStruct(elevation.shape, F32),
        ],
        in_specs=[vmem] * 5,
        out_specs=[vmem] * 3,
        scratch_shapes=[
            pltpu.VMEM((SLOT + 16, wide), F32),
            pltpu.VMEM((SLOT, wide), F32),
            pltpu.VMEM((SLOT, wide), F32),
        ],
        compiler_params=pltpu.CompilerParams(vmem_limit_bytes=24 * 1024 * 1024),
        name="update",
    )(*shared)


def solution(mesh):
    bands, sectors = mesh.shape["lat"], mesh.shape["lon"]
    return jax.shard_map(
        functools.partial(local, bands, sectors),
        mesh=mesh,
        in_specs=(
            P(None, "lat", "lon"),
            P(None, None, "lat", "lon"),
            P(None, "lat", "lon"),
            P("lat", "lon"),
            P("lat", "lon"),
            P(),
            P(),
        ),
        out_specs=(P(None, "lat", "lon"), P(None, None, "lat", "lon"), P(None, "lat", "lon")),
        check_vma=False,
    )
```

time: 59.3 us -> 45.2 us (0.76)
  Pallas kernels: 52.1 us -> 43.1 us
  local copies, waits for them, and re-layouts: 6.19 us -> 1.29 us
    pallas_call x1, Pallas kernels: 50.1 us -> 41.6 us  [local(): pl.pallas_call(functools.partial(spectral_kernel, bands, sectors, width,...]
    unnamed x12 -> x0, local copies, waits for them, and re-layouts: 5.48 us -> none
    reshape x1, local copies, waits for them, and re-layouts: 0.01 us -> 1.29 us  [local(): love_factor.reshape(1, DEGREES)]
    pad x1 -> x0, local copies, waits for them, and re-layouts: 0.7 us -> none  [local(): love = jnp.pad(love_factor, (0, length - DEGREES)).reshape(1, length)]
where the time goes in v2:
time: 45.2 us; the launch traced here: 45.1 us
  Pallas kernels  43.1 us (95%)
  local copies, waits for them, and re-layouts  1.29 us (3%)
  between operations  0.64 us (1%)
    pallas_call x1, Pallas kernels, local(): pl.pallas_call(functools.partial(spectral_kernel, bands, sectors, width,...  41.6 us
    pallas_call x1, Pallas kernels, local(): pl.pallas_call(functools.partial(update_kernel, bands, width, wide), out_...  1.56 us
    reshape x1, local copies, waits for them, and re-layouts, local(): love_factor.reshape(1, DEGREES)  1.29 us

profile of v2, /device:TPU:1, one launch (start us, length us, event | category | flops | bytes accessed | tf_op | source)
XLA Modules:
  0.0 45.1 jit_solution(15872972724321296376)
XLA Ops:
  0.6 1.3 %reshape.9.love = f32[1,1081]{1,0:T(1,128)} reshape(f32[1081]{0:T(1024)} %param.12) | data formatting | bytes 8648 | tf_op jit(solution)/shard_map/reshape | solution.py:453
  1.9 41.6 %spectral.1 = (f32[16,8,128]{2,1,0:T(8,128)S(1)}, bf16[128,1152]{1,0:T(8,128)(2,1)S(1)}, bf16[128,1152]{1,0:T(8,128)(2,1)S(1)}, f32[7,64,1152]{2,1,0:T(8,128)S(1)}, f32[64,128]{1,0:T(8,128)S(1)}) custom-call(f32[1,48,1080]{2,1,0:T(8,128)} %elevation.1, f32[1,2,48,1080]{3,2,1,0:T(8,128)} %velocity.1, f32[2,48,1080]{2,1,0:T(8,128)} %wind.1, f32[48,1080]{1,0:T(8,128)} %depth.1, ...), custom_call_target="tpu_custom_call" | custom-call | tf_op jit(solution)/shard_map/spectral/pallas_call | solution.py:402
  43.5 1.6 %update.1 = (f32[1,48,1080]{2,1,0:T(8,128)}, f32[1,2,48,1080]{3,2,1,0:T(8,128)}, f32[1,48,1080]{2,1,0:T(8,128)}) custom-call(f32[16,8,128]{2,1,0:T(8,128)S(1)} %get-tuple-element.8.spec, bf16[128,1152]{1,0:T(8,128)(2,1)S(1)} %get-tuple-element.9.th, bf16[128,1152]{1,0:T(8,128)(2,1)S(1)} %get-tuple-element.10.tl, ...), custom_call_target="tpu_custom_call" | custom-call | tf_op jit(solution)/shard_map/update/pallas_call | solution.py:455

commit v3 on v2

--- a/solution.py
+++ b/solution.py
@@ -21,7 +21,6 @@
 BF16 = jnp.bfloat16
 MESH = pl.DeviceIdType.MESH
 HBM = pltpu.MemorySpace.HBM
-SPLIT = 44
 
 
 def iota(shape, dim):
@@ -60,18 +59,20 @@
     bands, sectors, width, wide, length,
     elevation, velocity, wind, depth, mask, love, waves_hbm,
     out_spec, out_th, out_tl, out_fields, out_sine,
-    numbers, fields, mask_v, love_v, x_pad, part, part_in, place_out, place_in, coef, coef_in,
-    back_out, back_in, ring_out, row_msg, row_in, col_msg, col_in,
+    numbers, fields, mask_v, love_v, x_pad, part, pair_in, mine, piece_in, coef, coef_in,
+    back_out, row_msg, row_in, col_msg, col_in,
     ladder_v, ladder_s, raw, table_h, table_l, spec_in,
-    load_sem, rs_send, rs_recv, a_send, a_recv, c_send, c_recv,
-    s_send, s_recv, g_send, g_recv, h_send, h_recv,
+    load_sem, pair_send, pair_recv, a_send, a_recv, c_send, c_recv,
+    s_send, s_recv, last_send, last_recv, h_send, h_recv,
 ):
     depths = bands // PILE
-    ring = 2 * sectors
+    lows = sectors // 2
+    share = 4 * sectors
     band = lax.axis_index("lat")
     sector = lax.axis_index("lon")
     z, x, half = band // 8, (band // 2) % 4, band % 2
-    place = half * sectors + sector
+    low, core = sector // 2, sector % 2
+    place = (half * lows + low) * 4 + x
 
     sources = [
         (waves_hbm, numbers), (mask, mask_v), (elevation.at[0], fields.at[0]), (love, love_v),
@@ -87,13 +88,14 @@
     left = (band, (sector + sectors - 1) % sectors)
     right = (band, (sector + 1) % sectors)
 
-    def ring_peer(t):
-        return (z * 8 + x * 2 + t // sectors, t % sectors)
-
-    ring_peers = [ring_peer((place + d) % ring) for d in range(1, ring)]
-    x_peers = [(z * 8 + ((x + d) % 4) * 2 + half, sector) for d in range(1, 4)]
+    def chip(t):
+        y = t // 4
+        return (z * 8 + (t % 4) * 2 + y // lows, (y % lows) * 2 + core)
+
+    partner = (band, low * 2 + 1 - core)
+    chips = [chip((place + d) % share) for d in range(1, share)]
     z_peers = [(((z + d) % depths) * 8 + x * 2 + half, sector) for d in range(1, depths)]
-    peers = ring_peers + x_peers + z_peers + [above, below, left, right]
+    peers = [partner] + chips + z_peers + [above, below, left, right]
     barrier = pltpu.get_barrier_semaphore()
     for peer in peers:
         pl.semaphore_signal(barrier, inc=1, device_id=peer, device_id_type=MESH)
@@ -101,25 +103,26 @@
     loads[0].wait()
 
     lane = iota((1, 128), 1)
-    sub = iota((8, 128), 0)
+    sub = iota((16, 128), 0)
 
     def zonal(s, carry):
-        waves = jnp.zeros((8, 128), F32)
-        for p in range(8):
-            waves = jnp.where(sub == p, numbers[s * 8 + p].astype(F32), waves)
-        at = pl.multiple_of(s * 16, 16)
+        waves = jnp.zeros((16, 128), F32)
+        for p in range(16):
+            waves = jnp.where(sub == p, numbers[s * 16 + p].astype(F32), waves)
+        at = pl.multiple_of((s // (share // 16)) * 2 * share + (s % (share // 16)) * 16, 16)
         for tile in range(wide // 128):
             t = lane + tile * 128
             column = sector * width + jnp.where(t < width + 16, t, t - wide)
             cosine, sine = circle(waves * column.astype(F32), GRID_LON)
-            high, low = halves(
-                jnp.concatenate([cosine[0:4], sine[0:4], cosine[4:8], sine[4:8]], axis=0)
-            )
+            high, low_part = halves(cosine)
             out_th[pl.ds(at, 16), tile * 128 : tile * 128 + 128] = high
-            out_tl[pl.ds(at, 16), tile * 128 : tile * 128 + 128] = low
+            out_tl[pl.ds(at, 16), tile * 128 : tile * 128 + 128] = low_part
+            high, low_part = halves(sine)
+            out_th[pl.ds(at + share, 16), tile * 128 : tile * 128 + 128] = high
+            out_tl[pl.ds(at + share, 16), tile * 128 : tile * 128 + 128] = low_part
         return carry
 
-    lax.fori_loop(0, sectors, zonal, 0)
+    lax.fori_loop(0, share // 8, zonal, 0)
 
     x_pad[...] = jnp.zeros_like(x_pad)
     loads[1].wait()
@@ -130,10 +133,24 @@
     sums = (
         rows_dot_t(t_high, x_high) + rows_dot_t(t_high, x_low) + rows_dot_t(out_tl[...], x_high)
     )
-    for t in range(ring):
-        part[t] = sums[8 * t : 8 * t + 8]
-
-    number = numbers[place * 4 + x]
+    part[0] = sums[0 : 2 * share]
+    part[1] = sums[2 * share : 4 * share]
+
+    pl.semaphore_wait(barrier, len(peers))
+    sends = []
+
+    def send(src, dst, send_sem, recv_sem, peer):
+        copy = pltpu.make_async_remote_copy(
+            src_ref=src, dst_ref=dst, send_sem=send_sem, recv_sem=recv_sem,
+            device_id=peer, device_id_type=MESH,
+        )
+        copy.start()
+        sends.append(copy)
+        return copy
+
+    pair = send(part.at[1 - core], pair_in, pair_send.at[0], pair_recv.at[0], partner)
+
+    number = numbers[core * share + place]
     order = number.astype(F32)
     degree = (iota((16, 128), 0) * 128 + iota((16, 128), 1)).astype(F32)
     active = degree > order
@@ -148,24 +165,21 @@
     to_scalar = pltpu.make_async_copy(ladder_v, ladder_s, load_sem.at[len(sources)])
     to_scalar.start()
 
-    pl.semaphore_wait(barrier, len(peers))
-    sends = []
-
-    def send(src, dst, send_sem, recv_sem, peer):
-        copy = pltpu.make_async_remote_copy(
-            src_ref=src, dst_ref=dst, send_sem=send_sem, recv_sem=recv_sem,
-            device_id=peer, device_id_type=MESH,
-        )
-        copy.start()
-        sends.append(copy)
-        return copy
-
-    rs = [
-        send(part.at[(place + d) % ring], part_in.at[place], rs_send.at[d], rs_recv.at[d],
-             ring_peers[d - 1])
-        for d in range(1, ring)
+    slot_row = band * BAND - 8 + iota((1, SLOT), 1)
+    slot_sine = circle(slot_row.astype(F32) + 0.5, 2 * GRID_LAT)[1]
+    weights = slot_sine * (math.pi / (2.0 * GRID_LAT) / GRID_LON)
+    own = part[core]
+    pair.wait_recv()
+    total = (own + pair_in[...]) * weights
+    mine[0] = total[0:share]
+    mine[1] = total[share : 2 * share]
+    slot = 2 * x + half
+    moved = [
+        send(mine.at[:, (place + d) % share], piece_in.at[low, :, slot], a_send.at[d],
+             a_recv.at[d], chips[d - 1])
+        for d in range(1, share)
     ]
-    part_in[place] = part[place]
+    piece_in[low, :, pl.ds(slot, 1), :] = mine[:, pl.ds(place, 1), :]
 
     for i in range(3, len(sources)):
         loads[i].wait()
@@ -225,38 +239,16 @@
     zero = jnp.zeros((4, 128), F32)
     blocks = length // 16
     early = min(8, blocks)
-    middle = min(SPLIT, blocks)
     state = (zero, zero, log_scale)
     state = lax.fori_loop(0, early, functools.partial(block, True), state)
-    state = lax.fori_loop(early, middle, functools.partial(block, False), state)
-
-    for copy in rs:
-        copy.wait_recv()
-    pieces = []
-    for h in range(2):
-        total = part_in[h * sectors]
-        for s in range(1, sectors):
-            total = total + part_in[h * sectors + s]
-        pieces.append(total)
-    total = jnp.concatenate(pieces, axis=1)
-    slot_row = (z * 8 + x * 2 + lane // SLOT) * BAND - 8 + lane % SLOT
-    slot_sine = circle(slot_row.astype(F32) + 0.5, 2 * GRID_LAT)[1]
-    total = total * (slot_sine * (math.pi / (2.0 * GRID_LAT) / GRID_LON))
-    for p in range(4):
-        place_out[p, 0:1, :] = total[p : p + 1]
-        place_out[p, 1:2, :] = total[4 + p : 5 + p]
-    moved = [
-        send(place_out.at[(x + d) % 4], place_in.at[x], a_send.at[d], a_recv.at[d],
-             x_peers[d - 1])
-        for d in range(1, 4)
-    ]
-    place_in[x] = place_out[x]
-
-    lax.fori_loop(middle, blocks, functools.partial(block, False), state)
+    lax.fori_loop(early, blocks, functools.partial(block, False), state)
 
     for copy in moved:
         copy.wait_recv()
-    rows = jnp.concatenate([place_in[k] for k in range(4)], axis=1)
+    total = piece_in[0]
+    for s in range(1, lows):
+        total = total + piece_in[s]
+    rows = jnp.concatenate([total[:, k] for k in range(8)], axis=1)
     high = rows.astype(BF16).astype(F32)
     rows = jnp.concatenate([high, rows - high], axis=0).astype(BF16)
     product = rows_dot_t(rows, table_h[...]) + rows_dot_t(rows, table_l[...])
@@ -306,8 +298,8 @@
     whole = coef[...]
     for d in range(1, depths):
         whole = whole + coef_in[d]
-    degrees = love_v.shape[1]
-    weight = love_v[...] / (2.0 * iota((1, degrees), 1).astype(F32) + 1.0)
+    degrees = love_v.shape[0]
+    weight = love_v[...].reshape(1, degrees) / (2.0 * iota((1, degrees), 1).astype(F32) + 1.0)
     weight = jnp.concatenate([weight, jnp.zeros((1, length - degrees), F32)], axis=1)
     whole = whole * weight
     high = whole.astype(BF16).astype(F32)
@@ -317,25 +309,20 @@
     for k in range(4):
         back_out[k] = product[:, 128 * k : 128 * k + 128]
     returned = [
-        send(back_out.at[(x + d) % 4], back_in.at[x], s_send.at[d], s_recv.at[d], x_peers[d - 1])
-        for d in range(1, 4)
+        send(back_out.at[(x + d) % 4], spec_in.at[core, :, place], s_send.at[d], s_recv.at[d],
+             chips[d - 1])
+        for d in range(1, share)
     ]
-    back_in[x] = back_out[x]
+    spec_in[core, :, pl.ds(place, 1), :] = back_out[x].reshape(2, 1, 128)
     for copy in returned:
         copy.wait_recv()
-    for k in range(4):
-        ring_out[k : k + 1, :] = back_in[k, 0:1, :]
-        ring_out[4 + k : 5 + k, :] = back_in[k, 1:2, :]
-    spread = [
-        send(ring_out, spec_in.at[place], g_send.at[d], g_recv.at[d], ring_peers[d - 1])
-        for d in range(1, ring)
-    ]
-    spec_in[place] = ring_out[...]
-    for copy in spread:
-        copy.wait_recv()
-    out_spec[...] = spec_in[...]
-    for copy in sends:
+    last = send(spec_in.at[core], spec_in.at[core], last_send.at[0], last_recv.at[0], partner)
+    for copy in sends[:-1]:
         copy.wait_send()
+    out_spec[pl.ds(core, 1)] = spec_in[pl.ds(core, 1)].reshape(1, 2 * share, 128)
+    last.wait_recv()
+    out_spec[pl.ds(1 - core, 1)] = spec_in[pl.ds(1 - core, 1)].reshape(1, 2 * share, 128)
+    last.wait_send()
 
 
 def update_kernel(
@@ -395,16 +382,16 @@
     wide = -(-(width + 18) // 128) * 128
     length = -(-DEGREES // 16) * 16
     depths = bands // PILE
-    ring = 2 * sectors
+    share = 4 * sectors
     vmem = pl.BlockSpec(memory_space=pltpu.VMEM)
     hbm = pl.BlockSpec(memory_space=HBM)
     dma = pltpu.SemaphoreType.DMA
     shared = pl.pallas_call(
         functools.partial(spectral_kernel, bands, sectors, width, wide, length),
         out_shape=[
-            jax.ShapeDtypeStruct((ring, 8, 128), F32),
-            jax.ShapeDtypeStruct((8 * ring, wide), BF16),
-            jax.ShapeDtypeStruct((8 * ring, wide), BF16),
+            jax.ShapeDtypeStruct((2, 2 * share, 128), F32),
+            jax.ShapeDtypeStruct((4 * share, wide), BF16),
+            jax.ShapeDtypeStruct((4 * share, wide), BF16),
             jax.ShapeDtypeStruct((7, SLOT, wide), F32),
             jax.ShapeDtypeStruct((SLOT, 128), F32),
         ],
@@ -414,17 +401,15 @@
             pltpu.SMEM((8 * sectors,), jnp.int32),
             pltpu.VMEM((6, BAND, width), F32),
             pltpu.VMEM((BAND, width), jnp.int32),
-            pltpu.VMEM((1, DEGREES), F32),
+            pltpu.VMEM((DEGREES,), F32),
             pltpu.VMEM((SLOT, wide), F32),
-            pltpu.VMEM((ring, 8, SLOT), F32),
-            pltpu.VMEM((ring, 8, SLOT), F32),
-            pltpu.VMEM((4, 2, 128), F32),
-            pltpu.VMEM((4, 2, 128), F32),
+            pltpu.VMEM((2, 2 * share, SLOT), F32),
+            pltpu.VMEM((2 * share, SLOT), F32),
+            pltpu.VMEM((2, share, SLOT), F32),
+            pltpu.VMEM((sectors // 2, 2, 8, SLOT), F32),
             pltpu.VMEM((2, length), F32),
             pltpu.VMEM((depths, 2, length), F32),
             pltpu.VMEM((4, 2, 128), F32),
-            pltpu.VMEM((4, 2, 128), F32),
-            pltpu.VMEM((8, 128), F32),
             pltpu.VMEM((2, 8, width), F32),
             pltpu.VMEM((2, 8, width), F32),
             pltpu.VMEM((2, BAND, 128), F32),
@@ -434,13 +419,13 @@
             pltpu.VMEM((64, 128), F32),
             pltpu.VMEM((length, 512), BF16),
             pltpu.VMEM((length, 512), BF16),
-            pltpu.VMEM((ring, 8, 128), F32),
+            pltpu.VMEM((2, 2, share, 128), F32),
             dma((10,)),
-            dma((ring,)), dma((ring,)),
-            dma((4,)), dma((4,)),
+            dma((1,)), dma((1,)),
+            dma((share,)), dma((share,)),
             dma((depths,)), dma((depths,)),
-            dma((4,)), dma((4,)),
-            dma((ring,)), dma((ring,)),
+            dma((share,)), dma((share,)),
+            dma((1,)), dma((1,)),
             dma((4,)), dma((4,)),
         ],
         compiler_params=pltpu.CompilerParams(
@@ -450,7 +435,7 @@
     )(*[
         pltpu.with_memory_space_constraint(array, HBM)
         for array in (elevation, velocity, wind_forcing, ocean_depth, wet_mask,
-                      love_factor.reshape(1, DEGREES), wavenumbers)
+                      love_factor, wavenumbers)
     ])
     return pl.pallas_call(
         functools.partial(update_kernel, bands, width, wide),

time: 45.2 us -> 41.9 us (0.927)
  Pallas kernels: 43.1 us -> 41.2 us
  local copies, waits for them, and re-layouts: 1.29 us -> 0 us
    pallas_call x1, Pallas kernels: 41.6 us -> 39.6 us  [local(): pl.pallas_call(functools.partial(spectral_kernel, bands, sectors, width,...]
    reshape x1 -> x0, local copies, waits for them, and re-layouts: 1.29 us -> none  [local(): love_factor.reshape(1, DEGREES)]
where the time goes in v3:
time: 41.9 us; the launch traced here: 41.8 us
  Pallas kernels  41.2 us (98%)
  between operations  0.64 us (2%)
    pallas_call x1, Pallas kernels, local(): pl.pallas_call(functools.partial(spectral_kernel, bands, sectors, width,...  39.6 us
    pallas_call x1, Pallas kernels, local(): pl.pallas_call(functools.partial(update_kernel, bands, width, wide), out_...  1.56 us

profile of v3, /device:TPU:1, one launch (start us, length us, event | category | flops | bytes accessed | tf_op | source)
XLA Modules:
  0.0 41.8 jit_solution(16329379514009661535)
XLA Ops:
  0.6 39.6 %spectral.1 = (f32[2,64,128]{2,1,0:T(8,128)S(1)}, bf16[128,1152]{1,0:T(8,128)(2,1)S(1)}, bf16[128,1152]{1,0:T(8,128)(2,1)S(1)}, f32[7,64,1152]{2,1,0:T(8,128)S(1)}, f32[64,128]{1,0:T(8,128)S(1)}) custom-call(f32[1,48,1080]{2,1,0:T(8,128)} %elevation.1, f32[1,2,48,1080]{3,2,1,0:T(8,128)} %velocity.1, f32[2,48,1080]{2,1,0:T(8,128)} %wind.1, f32[48,1080]{1,0:T(8,128)} %depth.1, ...), custom_call_target="tpu_custom_call" | custom-call | tf_op jit(solution)/shard_map/spectral/pallas_call | solution.py:389
  40.3 1.6 %update.1 = (f32[1,48,1080]{2,1,0:T(8,128)}, f32[1,2,48,1080]{3,2,1,0:T(8,128)}, f32[1,48,1080]{2,1,0:T(8,128)}) custom-call(f32[2,64,128]{2,1,0:T(8,128)S(1)} %get-tuple-element.8.spec, bf16[128,1152]{1,0:T(8,128)(2,1)S(1)} %get-tuple-element.9.th, bf16[128,1152]{1,0:T(8,128)(2,1)S(1)} %get-tuple-element.10.tl, ...), custom_call_target="tpu_custom_call" | custom-call | tf_op jit(solution)/shard_map/update/pallas_call | solution.py:440

commit v4 on v3

--- a/solution.py
+++ b/solution.py
@@ -72,7 +72,6 @@
     sector = lax.axis_index("lon")
     z, x, half = band // 8, (band // 2) % 4, band % 2
     low, core = sector // 2, sector % 2
-    place = (half * lows + low) * 4 + x
 
     sources = [
         (waves_hbm, numbers), (mask, mask_v), (elevation.at[0], fields.at[0]), (love, love_v),
@@ -88,14 +87,23 @@
     left = (band, (sector + sectors - 1) % sectors)
     right = (band, (sector + 1) % sectors)
 
+    y = half * lows + low
+    place = y * 4 + x
+
     def chip(t):
-        y = t // 4
-        return (z * 8 + (t % 4) * 2 + y // lows, (y % lows) * 2 + core)
+        return (z * 8 + (t % 4) * 2 + t // 4 // lows, (t // 4 % lows) * 2 + core)
+
+    steps = sorted(
+        ((dy, dx) for dy in range(sectors) for dx in range(4) if dy or dx),
+        key=lambda s: -min(s[0], sectors - s[0]) - min(s[1], 4 - s[1]),
+    )
+    places = [((y + dy) % sectors) * 4 + (x + dx) % 4 for dy, dx in steps]
+    z_steps = sorted(range(1, depths), key=lambda d: -min(d, depths - d))
 
     partner = (band, low * 2 + 1 - core)
-    chips = [chip((place + d) % share) for d in range(1, share)]
-    z_peers = [(((z + d) % depths) * 8 + x * 2 + half, sector) for d in range(1, depths)]
-    peers = [partner] + chips + z_peers + [above, below, left, right]
+    chips = [chip(t) for t in places]
+    z_peers = [(((z + d) % depths) * 8 + x * 2 + half, sector) for d in z_steps]
+    peers = chips[:8] + z_peers + chips[8:] + [above, below, left, right, partner]
     barrier = pltpu.get_barrier_semaphore()
     for peer in peers:
         pl.semaphore_signal(barrier, inc=1, device_id=peer, device_id_type=MESH)
@@ -175,9 +183,8 @@
     mine[1] = total[share : 2 * share]
     slot = 2 * x + half
     moved = [
-        send(mine.at[:, (place + d) % share], piece_in.at[low, :, slot], a_send.at[d],
-             a_recv.at[d], chips[d - 1])
-        for d in range(1, share)
+        send(mine.at[:, t], piece_in.at[low, :, slot], a_send.at[n], a_recv.at[n], chips[n])
+        for n, t in enumerate(places)
     ]
     piece_in[low, :, pl.ds(slot, 1), :] = mine[:, pl.ds(place, 1), :]
 
@@ -251,12 +258,17 @@
     rows = jnp.concatenate([total[:, k] for k in range(8)], axis=1)
     high = rows.astype(BF16).astype(F32)
     rows = jnp.concatenate([high, rows - high], axis=0).astype(BF16)
-    product = rows_dot_t(rows, table_h[...]) + rows_dot_t(rows, table_l[...])
-    coef[...] = product[0:2] + product[2:4]
-    gathered = [
-        send(coef, coef_in.at[d], c_send.at[d], c_recv.at[d], z_peers[d - 1])
-        for d in range(1, depths)
-    ]
+    cut = min(512, length // 2 // 128 * 128)
+    parts = [slice(0, cut), slice(cut, length)] if cut else [slice(0, length)]
+    gathered = []
+    for h, part_rows in enumerate(parts):
+        product = rows_dot_t(rows, table_h[part_rows, :]) + rows_dot_t(rows, table_l[part_rows, :])
+        coef[:, part_rows] = product[0:2] + product[2:4]
+        gathered.append([
+            send(coef.at[:, part_rows], coef_in.at[d, :, part_rows], c_send.at[h, d],
+                 c_recv.at[h, d], peer)
+            for d, peer in zip(z_steps, z_peers)
+        ])
 
     for copy in rims:
         copy.wait_recv()
@@ -293,25 +305,28 @@
 
     lax.fori_loop(0, SLOT // 8, prepare, 0)
 
-    for copy in gathered:
-        copy.wait_recv()
-    whole = coef[...]
-    for d in range(1, depths):
-        whole = whole + coef_in[d]
     degrees = love_v.shape[0]
     weight = love_v[...].reshape(1, degrees) / (2.0 * iota((1, degrees), 1).astype(F32) + 1.0)
     weight = jnp.concatenate([weight, jnp.zeros((1, length - degrees), F32)], axis=1)
-    whole = whole * weight
-    high = whole.astype(BF16).astype(F32)
-    whole = jnp.concatenate([high, whole - high], axis=0).astype(BF16)
-    product = rows_dot(whole, table_h[...]) + rows_dot(whole, table_l[...])
+    product = 0.0
+    for part_rows, copies in zip(parts, gathered):
+        for copy in copies:
+            copy.wait_recv()
+        whole = coef[:, part_rows]
+        for d in range(1, depths):
+            whole = whole + coef_in[d, :, part_rows]
+        whole = whole * weight[:, part_rows]
+        high = whole.astype(BF16).astype(F32)
+        whole = jnp.concatenate([high, whole - high], axis=0).astype(BF16)
+        product = product + rows_dot(whole, table_h[part_rows, :])
+        product = product + rows_dot(whole, table_l[part_rows, :])
     product = product[0:2] + product[2:4]
     for k in range(4):
         back_out[k] = product[:, 128 * k : 128 * k + 128]
     returned = [
-        send(back_out.at[(x + d) % 4], spec_in.at[core, :, place], s_send.at[d], s_recv.at[d],
-             chips[d - 1])
-        for d in range(1, share)
+        send(back_out.at[t % 4], spec_in.at[core, :, place], s_send.at[n], s_recv.at[n],
+             chips[n])
+        for n, t in enumerate(places)
     ]
     spec_in[core, :, pl.ds(place, 1), :] = back_out[x].reshape(2, 1, 128)
     for copy in returned:
@@ -329,9 +344,17 @@
     bands, width, wide,
     spec, th, tl, fields, sine,
     new_elevation, new_velocity, loading,
-    surface, south_flux, loads,
+    surface, south_flux, loads, results, out_sem,
 ):
     band = lax.axis_index("lat")
+    copies = []
+
+    def store(index, target, rows):
+        copy = pltpu.make_async_copy(
+            results.at[index, rows], target.at[rows], out_sem.at[len(copies)]
+        )
+        copy.start()
+        copies.append(copy)
 
     source = iota((SLOT, 128), 0) + SLOT * (band % 2)
     move = jnp.where(iota((SLOT, 128), 1) == source, 1.0, 0.0).astype(BF16)
@@ -350,7 +373,8 @@
         load = loads[at, :]
         surface[8 + 8 * r : 16 + 8 * r, :] = jnp.where(inside, fields[0, at, :] - load, 0.0)
         if 1 <= r <= 6:
-            loading[0, 8 * r - 8 : 8 * r, :] = load[:, 0:width]
+            results[0, 8 * r - 8 : 8 * r, :] = load[:, 0:width]
+    store(0, loading.at[0], pl.ds(0, BAND))
     for r in range(8):
         at = slice(8 * r, 8 * r + 8)
         row = band * BAND - 8 + 8 * r + sub
@@ -360,7 +384,8 @@
         flux = sine[at, 0:1] * fields[5, at, :] * new_v
         south_flux[at, :] = jnp.where(inside, flux, 0.0)
         if 1 <= r <= 6:
-            new_velocity[0, 1, 8 * r - 8 : 8 * r, :] = new_v[:, 0:width]
+            results[1, 8 * r - 8 : 8 * r, :] = new_v[:, 0:width]
+    store(1, new_velocity.at[0, 1], pl.ds(0, BAND))
     for r in range(1, 7):
         at = slice(8 * r, 8 * r + 8)
         here = surface[8 + 8 * r : 16 + 8 * r, :]
@@ -372,8 +397,13 @@
         row_sine = sine[at, 0:1]
         tendency = (STEP_RATIO / row_sine) * east + (meridional / row_sine) * down
         level = fields[0, at, :] - fields[6, at, :] * tendency
-        new_velocity[0, 0, 8 * r - 8 : 8 * r, :] = new_u[:, 0:width]
-        new_elevation[0, 8 * r - 8 : 8 * r, :] = level[:, 0:width]
+        results[2, 8 * r - 8 : 8 * r, :] = new_u[:, 0:width]
+        results[3, 8 * r - 8 : 8 * r, :] = level[:, 0:width]
+        if r % 2 == 0:
+            store(2, new_velocity.at[0, 0], pl.ds(8 * r - 16, 16))
+            store(3, new_elevation.at[0], pl.ds(8 * r - 16, 16))
+    for copy in copies:
+        copy.wait()
 
 
 def local(bands, sectors, elevation, velocity, wind_forcing, ocean_depth, wet_mask, love_factor,
@@ -423,7 +453,7 @@
             dma((10,)),
             dma((1,)), dma((1,)),
             dma((share,)), dma((share,)),
-            dma((depths,)), dma((depths,)),
+            dma((2, depths)), dma((2, depths)),
             dma((share,)), dma((share,)),
             dma((1,)), dma((1,)),
             dma((4,)), dma((4,)),
@@ -445,11 +475,13 @@
             jax.ShapeDtypeStruct(elevation.shape, F32),
         ],
         in_specs=[vmem] * 5,
-        out_specs=[vmem] * 3,
+        out_specs=[hbm] * 3,
         scratch_shapes=[
             pltpu.VMEM((SLOT + 16, wide), F32),
             pltpu.VMEM((SLOT, wide), F32),
             pltpu.VMEM((SLOT, wide), F32),
+            pltpu.VMEM((4, BAND, width), F32),
+            dma((8,)),
         ],
         compiler_params=pltpu.CompilerParams(vmem_limit_bytes=24 * 1024 * 1024),
         name="update",

time: 41.9 us -> 39.9 us (0.952)
  Pallas kernels: 41.2 us -> 39.1 us
    pallas_call x1, Pallas kernels: 39.6 us -> 37.5 us  [local(): pl.pallas_call(functools.partial(spectral_kernel, bands, sectors, width,...]
where the time goes in v4:
time: 39.9 us; the launch traced here: 39.7 us
  Pallas kernels  39.1 us (98%)
  between operations  0.64 us (2%)
    pallas_call x1, Pallas kernels, local(): pl.pallas_call(functools.partial(spectral_kernel, bands, sectors, width,...  37.5 us
    pallas_call x1, Pallas kernels, local(): pl.pallas_call(functools.partial(update_kernel, bands, width, wide), out_...  1.58 us

profile of v4, /device:TPU:1, one launch (start us, length us, event | category | flops | bytes accessed | tf_op | source)
XLA Modules:
  0.0 39.7 jit_solution(11725827578350939842)
XLA Ops:
  0.6 37.5 %spectral.1 = (f32[2,64,128]{2,1,0:T(8,128)S(1)}, bf16[128,1152]{1,0:T(8,128)(2,1)S(1)}, bf16[128,1152]{1,0:T(8,128)(2,1)S(1)}, f32[7,64,1152]{2,1,0:T(8,128)S(1)}, f32[64,128]{1,0:T(8,128)S(1)}) custom-call(f32[1,48,1080]{2,1,0:T(8,128)} %elevation.1, f32[1,2,48,1080]{3,2,1,0:T(8,128)} %velocity.1, f32[2,48,1080]{2,1,0:T(8,128)} %wind.1, f32[48,1080]{1,0:T(8,128)} %depth.1, ...), custom_call_target="tpu_custom_call" | custom-call | tf_op jit(solution)/shard_map/spectral/pallas_call | solution.py:419
  38.2 1.6 %update.1 = (f32[1,48,1080]{2,1,0:T(8,128)}, f32[1,2,48,1080]{3,2,1,0:T(8,128)}, f32[1,48,1080]{2,1,0:T(8,128)}) custom-call(f32[2,64,128]{2,1,0:T(8,128)S(1)} %get-tuple-element.8.spec, bf16[128,1152]{1,0:T(8,128)(2,1)S(1)} %get-tuple-element.9.th, bf16[128,1152]{1,0:T(8,128)(2,1)S(1)} %get-tuple-element.10.tl, ...), custom_call_target="tpu_custom_call" | custom-call | tf_op jit(solution)/shard_map/update/pallas_call | solution.py:470

commit v5 on v4

--- a/solution.py
+++ b/solution.py
@@ -21,6 +21,7 @@
 BF16 = jnp.bfloat16
 MESH = pl.DeviceIdType.MESH
 HBM = pltpu.MemorySpace.HBM
+PRE = 8
 
 
 def iota(shape, dim):
@@ -59,11 +60,10 @@
     bands, sectors, width, wide, length,
     elevation, velocity, wind, depth, mask, love, waves_hbm,
     out_spec, out_th, out_tl, out_fields, out_sine,
-    numbers, fields, mask_v, love_v, x_pad, part, pair_in, mine, piece_in, coef, coef_in,
+    numbers, fields, mask_v, love_v, x_pad, part, piece_in, coef, coef_in,
     back_out, row_msg, row_in, col_msg, col_in,
     ladder_v, ladder_s, raw, table_h, table_l, spec_in,
-    load_sem, pair_send, pair_recv, a_send, a_recv, c_send, c_recv,
-    s_send, s_recv, last_send, last_recv, h_send, h_recv,
+    load_sem, a_send, a_recv, c_send, c_recv, s_send, s_recv, h_send, h_recv,
 ):
     depths = bands // PILE
     lows = sectors // 2
@@ -79,7 +79,7 @@
         (wind.at[0], fields.at[3]), (wind.at[1], fields.at[4]), (depth, fields.at[5]),
     ]
     loads = [pltpu.make_async_copy(a, b, load_sem.at[i]) for i, (a, b) in enumerate(sources)]
-    for copy in loads:
+    for copy in loads[:3]:
         copy.start()
 
     above = ((band + bands - 1) % bands, sector)
@@ -90,24 +90,28 @@
     y = half * lows + low
     place = y * 4 + x
 
-    def chip(t):
-        return (z * 8 + (t % 4) * 2 + t // 4 // lows, (t // 4 % lows) * 2 + core)
-
     steps = sorted(
-        ((dy, dx) for dy in range(sectors) for dx in range(4) if dy or dx),
+        ((dy, dx, dc) for dy in range(sectors) for dx in range(4) for dc in range(2)
+         if dy or dx or dc),
         key=lambda s: -min(s[0], sectors - s[0]) - min(s[1], 4 - s[1]),
     )
-    places = [((y + dy) % sectors) * 4 + (x + dx) % 4 for dy, dx in steps]
+    mates = []
+    for dy, dx, dc in steps:
+        peer_y, peer_x, peer_core = (y + dy) % sectors, (x + dx) % 4, (core + dc) % 2
+        peer = (z * 8 + peer_x * 2 + peer_y // lows, (peer_y % lows) * 2 + peer_core)
+        mates.append((peer, peer_core, peer_y * 4 + peer_x, peer_x))
     z_steps = sorted(range(1, depths), key=lambda d: -min(d, depths - d))
 
-    partner = (band, low * 2 + 1 - core)
-    chips = [chip(t) for t in places]
+    plane = [mate[0] for mate in mates]
     z_peers = [(((z + d) % depths) * 8 + x * 2 + half, sector) for d in z_steps]
-    peers = chips[:8] + z_peers + chips[8:] + [above, below, left, right, partner]
+    peers = plane[:20] + z_peers + plane[20:] + [above, below, left, right]
     barrier = pltpu.get_barrier_semaphore()
     for peer in peers:
         pl.semaphore_signal(barrier, inc=1, device_id=peer, device_id_type=MESH)
 
+    for copy in loads[3:]:
+        copy.start()
+    x_pad[...] = jnp.zeros_like(x_pad)
     loads[0].wait()
 
     lane = iota((1, 128), 1)
@@ -132,7 +136,6 @@
 
     lax.fori_loop(0, share // 8, zonal, 0)
 
-    x_pad[...] = jnp.zeros_like(x_pad)
     loads[1].wait()
     loads[2].wait()
     x_pad[8:56, 0:width] = fields[0] * mask_v[...].astype(F32)
@@ -141,8 +144,13 @@
     sums = (
         rows_dot_t(t_high, x_high) + rows_dot_t(t_high, x_low) + rows_dot_t(out_tl[...], x_high)
     )
-    part[0] = sums[0 : 2 * share]
-    part[1] = sums[2 * share : 4 * share]
+    slot_row = band * BAND - 8 + iota((1, SLOT), 1)
+    slot_sine = circle(slot_row.astype(F32) + 0.5, 2 * GRID_LAT)[1]
+    sums = sums * (slot_sine * (math.pi / (2.0 * GRID_LAT) / GRID_LON))
+    for c in range(2):
+        for kind in range(2):
+            at = (2 * c + kind) * share
+            part[c, kind] = sums[at : at + share]
 
     pl.semaphore_wait(barrier, len(peers))
     sends = []
@@ -156,7 +164,12 @@
         sends.append(copy)
         return copy
 
-    pair = send(part.at[1 - core], pair_in, pair_send.at[0], pair_recv.at[0], partner)
+    slot = 2 * x + half
+    moved = [
+        send(part.at[c, :, t], piece_in.at[sector, :, slot], a_send.at[n], a_recv.at[n], peer)
+        for n, (peer, c, t, _) in enumerate(mates)
+    ]
+    piece_in[sector, :, pl.ds(slot, 1), :] = part[core, :, pl.ds(place, 1), :]
 
     number = numbers[core * share + place]
     order = number.astype(F32)
@@ -172,21 +185,6 @@
     ladder_v[16:32, :] = raising * jnp.sqrt(under / over)
     to_scalar = pltpu.make_async_copy(ladder_v, ladder_s, load_sem.at[len(sources)])
     to_scalar.start()
-
-    slot_row = band * BAND - 8 + iota((1, SLOT), 1)
-    slot_sine = circle(slot_row.astype(F32) + 0.5, 2 * GRID_LAT)[1]
-    weights = slot_sine * (math.pi / (2.0 * GRID_LAT) / GRID_LON)
-    own = part[core]
-    pair.wait_recv()
-    total = (own + pair_in[...]) * weights
-    mine[0] = total[0:share]
-    mine[1] = total[share : 2 * share]
-    slot = 2 * x + half
-    moved = [
-        send(mine.at[:, t], piece_in.at[low, :, slot], a_send.at[n], a_recv.at[n], chips[n])
-        for n, t in enumerate(places)
-    ]
-    piece_in[low, :, pl.ds(slot, 1), :] = mine[:, pl.ds(place, 1), :]
 
     for i in range(3, len(sources)):
         loads[i].wait()
@@ -203,6 +201,7 @@
         col_msg[1, :, 2 * slot : 2 * slot + 2] = fields[index, :, width - 2 : width]
     col_msg[0, :, 10:12] = wet[:, 0:2]
     col_msg[1, :, 10:12] = wet[:, width - 2 : width]
+
     rims = [
         send(row_msg.at[0], row_in.at[1], h_send.at[0], h_recv.at[0], above),
         send(row_msg.at[1], row_in.at[0], h_send.at[1], h_recv.at[1], below),
@@ -248,12 +247,14 @@
     early = min(8, blocks)
     state = (zero, zero, log_scale)
     state = lax.fori_loop(0, early, functools.partial(block, True), state)
-    lax.fori_loop(early, blocks, functools.partial(block, False), state)
-
-    for copy in moved:
+    state = lax.fori_loop(early, min(PRE, blocks), functools.partial(block, False), state)
+
+    lax.fori_loop(min(PRE, blocks), blocks, functools.partial(block, False), state)
+
+    for copy in reversed(moved):
         copy.wait_recv()
     total = piece_in[0]
-    for s in range(1, lows):
+    for s in range(1, sectors):
         total = total + piece_in[s]
     rows = jnp.concatenate([total[:, k] for k in range(8)], axis=1)
     high = rows.astype(BF16).astype(F32)
@@ -304,13 +305,16 @@
         return carry
 
     lax.fori_loop(0, SLOT // 8, prepare, 0)
+    for copy in reversed(sends):
+        copy.wait_send()
+    sends.clear()
 
     degrees = love_v.shape[0]
     weight = love_v[...].reshape(1, degrees) / (2.0 * iota((1, degrees), 1).astype(F32) + 1.0)
     weight = jnp.concatenate([weight, jnp.zeros((1, length - degrees), F32)], axis=1)
     product = 0.0
     for part_rows, copies in zip(parts, gathered):
-        for copy in copies:
+        for copy in reversed(copies):
             copy.wait_recv()
         whole = coef[:, part_rows]
         for d in range(1, depths):
@@ -324,20 +328,16 @@
     for k in range(4):
         back_out[k] = product[:, 128 * k : 128 * k + 128]
     returned = [
-        send(back_out.at[t % 4], spec_in.at[core, :, place], s_send.at[n], s_recv.at[n],
-             chips[n])
-        for n, t in enumerate(places)
+        send(back_out.at[k], spec_in.at[core, :, place], s_send.at[n], s_recv.at[n], peer)
+        for n, (peer, _, _, k) in enumerate(mates)
     ]
     spec_in[core, :, pl.ds(place, 1), :] = back_out[x].reshape(2, 1, 128)
-    for copy in returned:
+    for copy in reversed(sends):
+        copy.wait_send()
+    for copy in reversed(returned):
         copy.wait_recv()
-    last = send(spec_in.at[core], spec_in.at[core], last_send.at[0], last_recv.at[0], partner)
-    for copy in sends[:-1]:
-        copy.wait_send()
-    out_spec[pl.ds(core, 1)] = spec_in[pl.ds(core, 1)].reshape(1, 2 * share, 128)
-    last.wait_recv()
-    out_spec[pl.ds(1 - core, 1)] = spec_in[pl.ds(1 - core, 1)].reshape(1, 2 * share, 128)
-    last.wait_send()
+    for c in range(2):
+        out_spec[c] = spec_in[c].reshape(2 * share, 128)
 
 
 def update_kernel(
@@ -433,10 +433,8 @@
             pltpu.VMEM((BAND, width), jnp.int32),
             pltpu.VMEM((DEGREES,), F32),
             pltpu.VMEM((SLOT, wide), F32),
-            pltpu.VMEM((2, 2 * share, SLOT), F32),
-            pltpu.VMEM((2 * share, SLOT), F32),
-            pltpu.VMEM((2, share, SLOT), F32),
-            pltpu.VMEM((sectors // 2, 2, 8, SLOT), F32),
+            pltpu.VMEM((2, 2, share, SLOT), F32),
+            pltpu.VMEM((sectors, 2, 8, SLOT), F32),
             pltpu.VMEM((2, length), F32),
             pltpu.VMEM((depths, 2, length), F32),
             pltpu.VMEM((4, 2, 128), F32),
@@ -451,11 +449,9 @@
             pltpu.VMEM((length, 512), BF16),
             pltpu.VMEM((2, 2, share, 128), F32),
             dma((10,)),
-            dma((1,)), dma((1,)),
-            dma((share,)), dma((share,)),
+            dma((2 * share,)), dma((2 * share,)),
             dma((2, depths)), dma((2, depths)),
-            dma((share,)), dma((share,)),
-            dma((1,)), dma((1,)),
+            dma((2 * share,)), dma((2 * share,)),
             dma((4,)), dma((4,)),
         ],
         compiler_params=pltpu.CompilerParams(

time: 39.9 us -> 39.5 us (0.990)
  Pallas kernels: 39.1 us -> 38.7 us
    pallas_call x1, Pallas kernels: 37.5 us -> 37.1 us  [local(): pl.pallas_call(functools.partial(spectral_kernel, bands, sectors, width,...]
where the time goes in v5:
time: 39.5 us; the launch traced here: 39.3 us
  Pallas kernels  38.7 us (98%)
  between operations  0.64 us (2%)
    pallas_call x1, Pallas kernels, local(): pl.pallas_call(functools.partial(spectral_kernel, bands, sectors, width,...  37.1 us
    pallas_call x1, Pallas kernels, local(): pl.pallas_call(functools.partial(update_kernel, bands, width, wide), out_...  1.58 us

profile of v5, /device:TPU:1, one launch (start us, length us, event | category | flops | bytes accessed | tf_op | source)
XLA Modules:
  0.0 39.3 jit_solution(16600328114961207556)
XLA Ops:
  0.6 37.1 %spectral.1 = (f32[2,64,128]{2,1,0:T(8,128)S(1)}, bf16[128,1152]{1,0:T(8,128)(2,1)S(1)}, bf16[128,1152]{1,0:T(8,128)(2,1)S(1)}, f32[7,64,1152]{2,1,0:T(8,128)S(1)}, f32[64,128]{1,0:T(8,128)S(1)}) custom-call(f32[1,48,1080]{2,1,0:T(8,128)} %elevation.1, f32[1,2,48,1080]{3,2,1,0:T(8,128)} %velocity.1, f32[2,48,1080]{2,1,0:T(8,128)} %wind.1, f32[48,1080]{1,0:T(8,128)} %depth.1, ...), custom_call_target="tpu_custom_call" | custom-call | tf_op jit(solution)/shard_map/spectral/pallas_call | solution.py:419
  37.8 1.6 %update.1 = (f32[1,48,1080]{2,1,0:T(8,128)}, f32[1,2,48,1080]{3,2,1,0:T(8,128)}, f32[1,48,1080]{2,1,0:T(8,128)}) custom-call(f32[2,64,128]{2,1,0:T(8,128)S(1)} %get-tuple-element.8.spec, bf16[128,1152]{1,0:T(8,128)(2,1)S(1)} %get-tuple-element.9.th, bf16[128,1152]{1,0:T(8,128)(2,1)S(1)} %get-tuple-element.10.tl, ...), custom_call_target="tpu_custom_call" | custom-call | tf_op jit(solution)/shard_map/update/pallas_call | solution.py:466

commit v6 on v5

--- a/solution.py
+++ b/solution.py
@@ -259,8 +259,8 @@
     rows = jnp.concatenate([total[:, k] for k in range(8)], axis=1)
     high = rows.astype(BF16).astype(F32)
     rows = jnp.concatenate([high, rows - high], axis=0).astype(BF16)
-    cut = min(512, length // 2 // 128 * 128)
-    parts = [slice(0, cut), slice(cut, length)] if cut else [slice(0, length)]
+    cut = max(128, length // 3 // 128 * 128 + 128)
+    parts = [slice(at, min(at + cut, length)) for at in range(0, length, cut)]
     gathered = []
     for h, part_rows in enumerate(parts):
         product = rows_dot_t(rows, table_h[part_rows, :]) + rows_dot_t(rows, table_l[part_rows, :])
@@ -450,7 +450,7 @@
             pltpu.VMEM((2, 2, share, 128), F32),
             dma((10,)),
             dma((2 * share,)), dma((2 * share,)),
-            dma((2, depths)), dma((2, depths)),
+            dma((3, depths)), dma((3, depths)),
             dma((2 * share,)), dma((2 * share,)),
             dma((4,)), dma((4,)),
         ],

time: 39.5 us -> 39.7 us (level)
  no operation moved by 1% of the time
where the time goes in v6:
time: 39.7 us; the launch traced here: 39.6 us
  Pallas kernels  39 us (98%)
  between operations  0.64 us (2%)
    pallas_call x1, Pallas kernels, local(): pl.pallas_call(functools.partial(spectral_kernel, bands, sectors, width,...  37.4 us
    pallas_call x1, Pallas kernels, local(): pl.pallas_call(functools.partial(update_kernel, bands, width, wide), out_...  1.58 us

profile of v6, /device:TPU:1, one launch (start us, length us, event | category | flops | bytes accessed | tf_op | source)
XLA Modules:
  0.0 39.6 jit_solution(14062175138817699802)
XLA Ops:
  0.6 37.4 %spectral.1 = (f32[2,64,128]{2,1,0:T(8,128)S(1)}, bf16[128,1152]{1,0:T(8,128)(2,1)S(1)}, bf16[128,1152]{1,0:T(8,128)(2,1)S(1)}, f32[7,64,1152]{2,1,0:T(8,128)S(1)}, f32[64,128]{1,0:T(8,128)S(1)}) custom-call(f32[1,48,1080]{2,1,0:T(8,128)} %elevation.1, f32[1,2,48,1080]{3,2,1,0:T(8,128)} %velocity.1, f32[2,48,1080]{2,1,0:T(8,128)} %wind.1, f32[48,1080]{1,0:T(8,128)} %depth.1, ...), custom_call_target="tpu_custom_call" | custom-call | tf_op jit(solution)/shard_map/spectral/pallas_call | solution.py:419
  38.0 1.6 %update.1 = (f32[1,48,1080]{2,1,0:T(8,128)}, f32[1,2,48,1080]{3,2,1,0:T(8,128)}, f32[1,48,1080]{2,1,0:T(8,128)}) custom-call(f32[2,64,128]{2,1,0:T(8,128)S(1)} %get-tuple-element.8.spec, bf16[128,1152]{1,0:T(8,128)(2,1)S(1)} %get-tuple-element.9.th, bf16[128,1152]{1,0:T(8,128)(2,1)S(1)} %get-tuple-element.10.tl, ...), custom_call_target="tpu_custom_call" | custom-call | tf_op jit(solution)/shard_map/update/pallas_call | solution.py:466
